TPU v7x, 128 devices: a whole 4x4x4 slice. The times are simulated.
128 devices in a mesh: stn: 16 (over x, z), img: 8 (over y, core).
Axes of the slice: x: 4, y: 4, z: 4, core: 2. Of those that a mesh axis runs over, the one named last changes fastest.
Arguments:
- voltages: float32 [2, 512, 256, 384], P(None, 'stn', 'img'), may hold values from -6 to 6
- prototype: float32 [4, 384], replicated, may hold values from -3 to 3
- uv_cells: float32 [2, 5242880], P(None, ('stn', 'img')), may hold values from -16 to 16
- w_cells: float32 [5242880], P(('stn', 'img')), may hold values from -8 to 8
- subgrid_of: int32 [5242880, 1], P(('stn', 'img')), may hold values from 0 to 1023; in each aligned block of 40960 rows (0 to 40959, 40960 to 81919, ...) at most 80 rows name the same one
Outputs:
- visibilities: float32 [128, 10, 2, 128, 128], P(('stn', 'img'))
- subgrids: float32 [1024, 2, 1024], P(('stn', 'img'))
Inputs may be any that keep to these rules, and one draw needn't show every extreme that they name: `subgrid_of`: of the records of one device (aligned blocks of 40960), at most 80 go to one subgrid, and some subgrid gets exactly 80 of them.
All inputs are finite; a program needn't handle non-finite values.
Results may differ from a plain program's by a relative error of at most 0.0003.
Values sent between devices are 32-bit elements; how exact they have to be, the bound alone decides.
No kernel may reach another device: no remote copies, remote signals or barrier semaphores. Data moves between devices by JAX's collectives and lax.ppermute only.
A program may use at most 192 MiB of HBM per device.

v0:
```python
import math

import jax
import jax.numpy as jnp
from jax import lax
from jax.sharding import PartitionSpec as P

TILE = 64
SUBGRID = 32
CH_DEV = 1
SUB_DEV = 8


HIGH = lax.Precision.HIGHEST


def shifted(block, axis, distance):
    devices = range(lax.axis_size(axis))
    route = [(i - distance, i) for i in devices if i - distance in devices]
    return lax.ppermute(block, axis, route)


def correlate(spectra):
    samples = spectra.shape[3]
    width_in = 2 * TILE
    tile_count = spectra.shape[2] // width_in
    blocks = []
    for tile_row in range(tile_count):
        real_rows = spectra[0, :, tile_row * width_in : (tile_row + 1) * width_in]
        imag_rows = spectra[1, :, tile_row * width_in : (tile_row + 1) * width_in]
        left_side = jnp.concatenate(
            [
                jnp.concatenate([real_rows, imag_rows], 2),
                jnp.concatenate([imag_rows, -real_rows], 2),
            ],
            1,
        )
        right_side = jnp.concatenate(
            [
                spectra[0, :, : (tile_row + 1) * width_in],
                spectra[1, :, : (tile_row + 1) * width_in],
            ],
            2,
        )
        product = jnp.einsum("cas,cbs->cab", left_side, right_side, precision=HIGH) / samples
        chans = product.shape[0]
        product = product.reshape(chans, 2, width_in, tile_row + 1, width_in).transpose(
            0, 3, 1, 2, 4
        )
        blocks.append(product)
    return jnp.concatenate(blocks, 1)


def stokes_of(visible):
    return 0.5 * (visible[..., 0::2, 0::2] + visible[..., 1::2, 1::2])


def phase_table(coord, wterm):
    centre = (jnp.arange(SUBGRID, dtype=jnp.float32) - (SUBGRID - 1) / 2.0) / SUBGRID
    angle = (
        2.0 * jnp.pi * centre[:, None] * coord[None, :]
        - jnp.pi * (centre * centre)[:, None] * wterm[None, :]
    )
    return (jnp.cos(angle), jnp.sin(angle))


def grid_one(fields):
    cos_left, sin_left = phase_table(fields[2], fields[3 + 1])
    cos_right, sin_right = phase_table(fields[3], fields[3 + 1])
    real_left = fields[0][None, :] * cos_left - fields[1][None, :] * sin_left
    imag_left = fields[0][None, :] * sin_left + fields[1][None, :] * cos_left
    left_side = jnp.concatenate([real_left, imag_left], 0)
    right_side = jnp.concatenate([cos_right, sin_right], 0)
    joined = lax.dot_general(left_side, right_side, (((1,), (1,)), ((), ())), precision=HIGH)
    width = SUBGRID
    real_grid = joined[:width, :width] - joined[width:, width:]
    imag_grid = joined[:width, width:] + joined[width:, :width]
    return jnp.stack([real_grid.reshape(-1), imag_grid.reshape(-1)])


def pack_records(fields, targets, nsub, most):
    total = targets.shape[0]
    order = jnp.argsort(targets, stable=True)
    ranked = targets[order]
    counts = jax.ops.segment_sum(jnp.ones_like(targets), targets, num_segments=nsub)
    starts = jnp.cumsum(counts) - counts
    within = jnp.arange(total, dtype=jnp.int32) - starts[ranked]
    slots = jnp.zeros((total,), jnp.int32).at[order].set(ranked * most + within)
    return jnp.zeros((fields.shape[0], nsub * most), fields.dtype).at[:, slots].set(fields)


def dft_table(length, used):
    index_k = jnp.arange(length, dtype=jnp.int32)
    index_c = jnp.arange(used, dtype=jnp.int32)
    wrapped = index_k[:, None] * index_c[None, :] % length
    angle = 2.0 * math.pi / length * wrapped.astype(jnp.float32)
    scale = 1.0 / math.sqrt(length)
    cosine = jnp.cos(angle) * scale
    sine = jnp.sin(angle) * scale
    return jnp.stack([jnp.stack([cosine, -sine], 1), jnp.stack([sine, cosine], 1)], 0)


def grid_items(received):
    item_count = received.shape[2]
    moved = jnp.moveaxis(received, 2, 0).reshape(item_count, 5, -1)
    return lax.map(grid_one, moved)


def per_device(voltages, prototype, uv_cells, w_cells, subgrid_of):
    taps = prototype.shape[0]
    length = prototype.shape[1]
    spec_dev = voltages.shape[2]
    inputs_dev = voltages.shape[1]
    stn_count = lax.axis_size("stn")
    img_count = lax.axis_size("img")
    devices = stn_count * img_count
    tail = voltages[:, :, spec_dev - (taps - 1) :, :]
    earlier = shifted(tail, "img", 1)
    extended = jnp.concatenate([earlier, voltages], 2)
    filtered = prototype[0] * extended[:, :, 0:spec_dev, :]
    for tap_index in range(1, taps):
        filtered = (
            filtered + prototype[tap_index] * extended[:, :, tap_index : tap_index + spec_dev, :]
        )
    corr_ch = CH_DEV * devices
    table = dft_table(length, corr_ch)
    spectra = jnp.einsum("pkqc,pisk->qcis", table, filtered, precision=HIGH)
    expanded = spectra[:, None]
    arrived = lax.all_to_all(expanded, ("stn", "img"), split_axis=2, concat_axis=1, tiled=True)
    arrived = arrived.reshape(2, stn_count, img_count, CH_DEV, inputs_dev, spec_dev)
    local = arrived.transpose(0, 3, 1, 4, 2, 5).reshape(
        2, CH_DEV, stn_count * inputs_dev, img_count * spec_dev
    )
    visibilities = correlate(local)
    stokes = stokes_of(visibilities)
    fields = jnp.stack(
        [
            stokes[:, :, 0].reshape(-1),
            stokes[:, :, 1].reshape(-1),
            uv_cells[0],
            uv_cells[1],
            w_cells,
        ]
    )
    vis_dev = fields.shape[1]
    nsub = SUB_DEV * devices
    most = 2 * vis_dev // nsub
    packed = pack_records(fields, subgrid_of[:, 0], nsub, most)
    outgoing = packed.reshape(5, devices, SUB_DEV, most)
    subgrids = grid_items(
        lax.all_to_all(outgoing, ("stn", "img"), split_axis=1, concat_axis=1, tiled=True)
    )
    return (visibilities, subgrids)


def solution(mesh):
    placed = (
        P(None, "stn", "img", None),
        P(),
        P(None, ("stn", "img")),
        P(("stn", "img")),
        P(("stn", "img"), None),
    )
    return jax.shard_map(
        per_device,
        mesh=mesh,
        in_specs=placed,
        out_specs=(P(("stn", "img"), None, None, None, None), P(("stn", "img"), None, None)),
        check_vma=False,
    )
```

profile of v0, /device:TPU:1, one launch (start us, length us, event | category | flops | bytes accessed | tf_op | source)
XLA Modules:
  0.0 1262.9 jit_solution(4005212426332055978)
XLA Ops:
  7.3 283.3 %scatter_custom_fusion = s32[1024]{0:T(1024)S(1)} fusion(s32[40960]{0:T(1024)} %bitcast.143, s32[40960]{0:T(1024)S(1)} %broadcast.199, s32[]{:T(128)} %constant.75.clone.1), kind=kCustom, calls=%fused_computation.138 | custom fusion | flops 40960 | bytes 4608 | tf_op jit(solution)/shard_map/scatter-add | solution.py:85
  291.2 26.1 %sort.17 = (s32[40960]{0:T(1024)}, s32[40960]{0:T(1024)S(1)}) sort(s32[40960]{0:T(1024)} %bitcast.144, s32[40960]{0:T(1024)S(1)} %iota.49), dimensions={0}, to_apply=%region_0.1 | sort | flops 655360 | bytes 655360 | tf_op jit(solution)/shard_map/jit(argsort)/sort | solution.py:83
  317.4 225.5 %gather_fusion = s32[40960]{0:T(1024)S(1)} fusion(s32[40960]{0:T(1024)S(1)} %bitcast.145, s32[40960]{0:T(1024)S(1)} %get-tuple-element.96), kind=kCustom, calls=%fused_computation | custom fusion | bytes 491520 | tf_op jit(solution)/shard_map/gather | solution.py:84
  543.2 162.4 %gather_fusion.1 = s32[40960]{0:T(1024)S(1)} fusion(s32[1024]{0:T(1024)S(1)} %bitcast_subtract_fusion, s32[40960]{0:T(1024)S(1)} %broadcast_clamp_fusion), kind=kCustom, calls=%fused_computation.1 | custom fusion | bytes 491520 | tf_op jit(solution)/shard_map/gather | solution.py:87
  705.7 150.0 %scatter_custom_fusion.1 = s32[40960]{0:T(1024)S(1)} fusion(s32[40960]{0:T(1024)S(1)} %get-tuple-element.97, s32[40960]{0:T(1024)S(1)} %subtract_add_fusion, s32[]{:T(128)} %constant.75.clone.1), kind=kCustom, calls=%fused_computation.134 | custom fusion | bytes 163844 | tf_op jit(solution)/shard_map/scatter | solution.py:88
  856.8 7.6 fusion.27
  873.5 10.3 all-to-all-start
  883.9 18.9 %all-to-all-done = f32[128,1,2048]{2,1,0:T(1,128)S(1)} async-done(((f32[128,1,2048]{2,1,0:T(1,128)}), f32[128,1,2048]{2,1,0:T(1,128)S(1)}, u32[]{:S(2)}, u32[]{:S(2)}) %all-to-all-start) | async-done | bytes 1048608 | tf_op jit(solution)/shard_map/all_to_all | solution.py:129
  913.8 5.8 copy.39
  942.2 11.6 slice.178
  953.8 11.9 slice.179
  966.9 10.0 copy.52
  976.9 116.8 %scatter_custom_fusion.2 = f32[5,81920]{0,1:T(8,128)} fusion(s32[40960]{0:T(1024)S(1)} %compare_select_fusion.1, f32[40960,5]{1,0:T(8,128)} %copy.52, f32[]{:T(128)} %constant.79.clone.1), kind=kCustom, calls=%fused_computation.33 | custom fusion | bytes 1638912 | tf_op jit(solution)/shard_map/scatter | solution.py:89
  1093.7 23.2 %copy.53 = f32[5,128,8,80]{3,2,0,1:T(8,128)} copy(f32[5,128,8,80]{0,3,2,1:T(8,128)} %bitcast.146) | data formatting | bytes 3276800 | tf_op jit(solution)/shard_map/reshape | solution.py:149
  1122.0 36.0 %all-to-all-done.1 = f32[5,128,8,80]{3,2,0,1:T(8,128)S(1)} async-done(((f32[5,128,8,80]{3,2,0,1:T(8,128)}), f32[5,128,8,80]{3,2,0,1:T(8,128)S(1)}, u32[]{:S(2)}, u32[]{:S(2)}) %all-to-all-start.1) | async-done | bytes 1638432 | tf_op jit(solution)/shard_map/all_to_all | solution.py:151
  1163.4 98.7 %while.12 = (s32[]{:T(128)}, f32[8,2,1024]{2,1,0:T(2,128)S(1)}, f32[8,5,10240]{2,1,0:T(8,128)S(1)}, s32[]{:T(128)}, s32[]{:T(128)}, /*index=5*/s32[]{}, s32[]{}, s32[]{}, s32[]{}) while((s32[]{:T(128)}, f32[8,2,1024]{2,1,0:T(2,128)S(1)}, f32[8,5,10240]{2,1,0:T(8,128)S(1)}, s32[]{:T(128)}, s32[]{:T(128)}, /*index=5*/s32[]{}, s32[]{}, s32[]{}, ...), condition=%wide.region_7.8_spmd, body=%wide.region_6.7_spmd.sunk | while | flops 508235936 | bytes 11174565 | solution.py:106
  1163.6 9.6 fusion.94
  1175.9 9.6 fusion.94
  1188.3 9.6 fusion.94
  1200.6 9.6 fusion.94
  1212.9 9.6 fusion.94
  1225.3 9.6 fusion.94
  1237.6 9.6 fusion.94
  1249.9 9.6 fusion.94
  (139 shorter events, 84.8 us)
Async XLA Ops:
  0.6 316.7 %copy-start = (s32[40960,1]{0,1:T(1,128)S(1)}, s32[40960,1]{0,1:T(1,128)}, u32[]{:S(2)}) copy-start(s32[40960,1]{0,1:T(1,128)} %param.11) | copy-start | bytes 491524
  1.9 854.7 %collective-permute-start = (f32[2,32,3,384]{3,1,2,0:T(8,128)S(1)}, f32[2,32,3,384]{3,1,2,0:T(8,128)S(1)}, u32[]{:S(2)}, u32[]{:S(2)}) collective-permute-start(f32[2,32,3,384]{3,1,2,0:T(8,128)S(1)} %copy.60), channel_id=1, source_target_pairs={{0,1},{1,2},{2,3},{3,4},{4,5},{5,6},{6,7},{8,9},{9,10},{10,11},{11... | collective-permute-start | bytes 884744 | tf_op jit(solution)/shard_map/ppermute | solution.py:20
  543.1 162.5 %copy-start.9 = (f32[4,384]{1,0:T(4,128)S(1)}, f32[4,384]{1,0:T(4,128)}, u32[]{:S(2)}) copy-start(f32[4,384]{1,0:T(4,128)} %param.8) | copy-start | bytes 18436
  873.5 29.3 %all-to-all-start = ((f32[128,1,2048]{2,1,0:T(1,128)}), f32[128,1,2048]{2,1,0:T(1,128)S(1)}, u32[]{:S(2)}, u32[]{:S(2)}) async-start(f32[128,1,2048]{2,1,0:T(1,128)} %reshape.323), calls=%async_computation | async-start | bytes 2097152 | tf_op jit(solution)/shard_map/all_to_all | solution.py:129
  911.9 1.9 copy-start.1
  923.1 2.4 copy-start.2
  938.8 2.6 copy-start.6
  938.8 2.7 copy-start.7
  938.8 2.7 copy-start.8
  942.2 23.7 %copy-start.3 = (f32[1,10,2,128,128]{4,3,2,1,0:T(8,128)}, f32[1,10,2,128,128]{4,3,2,1,0:T(8,128)S(1)}, u32[]{:S(2)}) copy-start(f32[1,10,2,128,128]{4,3,2,1,0:T(8,128)S(1)} %pad_maximum_fusion.1) | copy-start | bytes 3932164
  953.8 12.5 copy-start.4
  953.8 12.5 copy-start.5
  1117.0 41.1 %all-to-all-start.1 = ((f32[5,128,8,80]{3,2,0,1:T(8,128)}), f32[5,128,8,80]{3,2,0,1:T(8,128)S(1)}, u32[]{:S(2)}, u32[]{:S(2)}) async-start(f32[5,128,8,80]{3,2,0,1:T(8,128)} %copy.53), calls=%async_computation.1 | async-start | bytes 5242880 | tf_op jit(solution)/shard_map/all_to_all | solution.py:151
  1262.0 0.6 copy-start.10
where the time goes:
time: 1270 us; the launch traced here: 1260 us
  local copies, waits for them, and re-layouts  762 us (60%)
  other arithmetic  394 us (31%)
  waiting for transfers between devices  55 us (4%)
  matrix products  29.9 us (2%)
  starting transfers between devices  20 us (2%)
    scatter-add x1, other arithmetic, pack_records(): jax.ops.segment_sum(jnp.ones_like(targets), targets, num_segments=nsub)  283 us
    gather x1, local copies, waits for them, and re-layouts, pack_records(): ranked = targets[order]  226 us
    gather x1, local copies, waits for them, and re-layouts, pack_records(): within = jnp.arange(total, dtype=jnp.int32) - starts[ranked]  162 us
    scatter x1, local copies, waits for them, and re-layouts, pack_records(): slots = jnp.zeros((total,), jnp.int32).at[order].set(ranked * most + within)  150 us
    scatter x1, local copies, waits for them, and re-layouts, pack_records(): jnp.zeros((fields.shape[0], nsub * most), fields.dtype).at[:, slots]  117 us
    cos x8, other arithmetic, phase_table(): return (jnp.cos(angle), jnp.sin(angle))  76.8 us
    all_to_all x1, waiting for transfers between devices, per_device(): lax.all_to_all(outgoing, ('stn', 'img'), split_axis=1, concat_axis=1, til...  36 us
    sort x1, other arithmetic, pack_records(): order = jnp.argsort(targets, stable=True)  26.1 us
  transfers between devices with their start and end apart: 3, of which 2 were waited for; matrix products, arithmetic and copies ran while one was open for 67% of the time, Pallas kernels for 0%

commit v1 on v0

v1 whole, which is shorter than its diff:
```python
import functools
import math

import jax
import jax.numpy as jnp
import ml_dtypes
import numpy as np
from jax import lax
from jax.experimental import pallas as pl
from jax.experimental.pallas import tpu as pltpu
from jax.sharding import PartitionSpec as P

F32 = jnp.float32
BF16 = jnp.bfloat16
I32 = jnp.int32
VMEM = pltpu.VMEM
SMEM = pltpu.SMEM
NT = (((1,), (1,)), ((), ()))
NN = (((1,), (0,)), ((), ()))
AXES = ("stn", "img")


def split_bf16(x):
    high = x.astype(BF16)
    return high, (x - high.astype(F32)).astype(BF16)


def dot_nt(a, b):
    return lax.dot_general(a, b, NT, preferred_element_type=F32)


def dft_rows():
    k = np.arange(384)
    c = np.arange(128)
    angle = 2.0 * np.pi / 384 * ((c[:, None] * k[None, :]) % 384)
    cosine = np.cos(angle) / math.sqrt(384)
    sine = np.sin(angle) / math.sqrt(384)
    table = np.concatenate(
        [np.concatenate([cosine, sine], 1), np.concatenate([-sine, cosine], 1)], 0
    ).astype(np.float32)
    high = table.astype(ml_dtypes.bfloat16)
    low = (table - high.astype(np.float32)).astype(ml_dtypes.bfloat16)
    return high, low


def channel_kernel(volt, halo, proto, table_high, table_low, out, ext, fh, fl):
    step = pl.program_id(0)
    for p in range(2):
        for kt in range(3):
            lanes = slice(kt * 128, (kt + 1) * 128)
            for a in range(3):
                ext[kt, pl.ds(p * 320 + 5 + a, 8, stride=40), :] = halo[p, a, :, lanes]
            for i in range(8):
                base = (p * 8 + i) * 40 + 8
                ext[kt, base : base + 32, :] = volt[p, i, :, lanes]
    for half in range(2):
        for p in range(2):
            for kt in range(3):
                lanes = slice(kt * 128, (kt + 1) * 128)
                cols = slice(p * 384 + kt * 128, p * 384 + (kt + 1) * 128)
                for i in range(4):
                    base = (p * 8 + half * 4 + i) * 40 + 5
                    total = proto[0:1, lanes] * ext[kt, base : base + 32, :]
                    for a in range(1, 4):
                        total = total + proto[a : a + 1, lanes] * ext[kt, base + a : base + a + 32, :]
                    high, low = split_bf16(total)
                    fh[half, i * 32 : (i + 1) * 32, cols] = high
                    fl[half, i * 32 : (i + 1) * 32, cols] = low
        high = fh[half]
        result = (
            dot_nt(table_high[...], high)
            + dot_nt(table_high[...], fl[half])
            + dot_nt(table_low[...], high)
        )
        row = step * 2 + half
        out[pl.ds(row, 128, stride=16), :] = result[:128]
        out[pl.ds(8 + row, 128, stride=16), :] = result[128:]


def channelize(voltages, halo, prototype):
    high, low = dft_rows()
    whole = lambda shape: pl.BlockSpec(shape, lambda j: (0,) * len(shape))
    return pl.pallas_call(
        channel_kernel,
        grid=(4,),
        in_specs=[
            pl.BlockSpec((2, 8, 32, 384), lambda j: (0, j, 0, 0)),
            pl.BlockSpec((2, 3, 8, 384), lambda j: (0, 0, j, 0)),
            whole((4, 384)),
            whole((256, 768)),
            whole((256, 768)),
        ],
        out_specs=whole((2048, 128)),
        out_shape=jax.ShapeDtypeStruct((2048, 128), F32),
        scratch_shapes=[
            VMEM((3, 640, 128), F32),
            VMEM((2, 128, 768), BF16),
            VMEM((2, 128, 768), BF16),
        ],
        compiler_params=pltpu.CompilerParams(vmem_limit_bytes=40 << 20),
        cost_estimate=pl.CostEstimate(flops=1200000000, bytes_accessed=6000000, transcendentals=0),
        name="channelizer",
    )(voltages, halo, prototype, jnp.asarray(high), jnp.asarray(low))


def correlate_kernel(recv, vis, stokes, a_ref, hh, hl, xlh, xll, xrh, xrl):
    lane = lax.broadcasted_iota(I32, (8, 128), 1) >> 5

    def turn(stn, carry):
        for h in range(2):
            for q in range(2):
                parts = []
                for m in range(4):
                    row = pl.multiple_of(stn * 128 + (h * 4 + m) * 16 + q * 8, 8)
                    parts.append(recv[pl.ds(row, 8), :])
                for b in range(4):
                    joined = None
                    for m in range(4):
                        shift = (32 * (m - b)) % 128
                        moved = pltpu.roll(parts[m], shift, 1) if shift else parts[m]
                        joined = moved if joined is None else jnp.where(lane == m, moved, joined)
                    a_ref[q, h, pl.ds(stn * 32 + b, 8, stride=4), :] = joined
        return carry

    lax.fori_loop(0, 16, turn, 0)

    for q in range(2):
        for h in range(2):
            cols = slice((q * 2 + h) * 128, (q * 2 + h + 1) * 128)
            high, low = split_bf16(a_ref[q, h])
            hh[:, cols] = high
            hl[:, cols] = low
            for pol in range(2):
                cols = slice(((q * 2 + pol) * 2 + h) * 128, ((q * 2 + pol) * 2 + h + 1) * 128)
                for r in range(4):
                    for par in range(2):
                        start = 128 * r + 2 * par + pol
                        high, low = split_bf16(a_ref[q, h, pl.ds(start, 32, stride=4), :])
                        rows = slice(r * 64 + par * 32, r * 64 + par * 32 + 32)
                        xlh[rows, cols] = high
                        xll[rows, cols] = low
                    high, low = split_bf16(a_ref[q, h, pl.ds(128 * r + pol, 64, stride=2), :])
                    for twice in range(2):
                        rows = slice(r * 128 + twice * 64, r * 128 + twice * 64 + 64)
                        xrh[rows, cols] = high
                        xrl[rows, cols] = low

    def both(ref, rows):
        block = ref[rows, :]
        half = block.shape[1] // 2
        turned = jnp.concatenate([block[:, half:], -block[:, :half]], 1)
        return jnp.concatenate([block, turned], 0)

    lane128 = lax.broadcasted_iota(I32, (32, 128), 1)
    for r in range(4):
        width = (r + 1) * 128
        rows = slice(r * 128, (r + 1) * 128)
        left_high = both(hh, rows)
        left_low = both(hl, rows)
        right_high = hh[0:width, :]
        result = (
            dot_nt(left_high, right_high)
            + dot_nt(left_high, hl[0:width, :])
            + dot_nt(left_low, right_high)
        ) * (1.0 / 256.0)
        rows = slice(r * 64, (r + 1) * 64)
        left_high = both(xlh, rows)
        left_low = both(xll, rows)
        right_high = xrh[0:width, :]
        summed = (
            dot_nt(left_high, right_high)
            + dot_nt(left_high, xrl[0:width, :])
            + dot_nt(left_low, right_high)
        ) * (1.0 / 512.0)
        for s in range(r + 1):
            pair = r * (r + 1) // 2 + s
            cols = slice(s * 128, (s + 1) * 128)
            vis[pair, 0] = result[0:128, cols]
            vis[pair, 1] = result[128:256, cols]
            for q in range(2):
                even = summed[q * 64 : q * 64 + 32, cols]
                odd = summed[q * 64 + 32 : q * 64 + 64, cols]
                stokes[q, pair * 32 : (pair + 1) * 32, :] = jnp.where(lane128 < 64, even, odd)


def correlate(recv):
    spec = pl.BlockSpec(memory_space=VMEM)
    return pl.pallas_call(
        correlate_kernel,
        in_specs=[spec],
        out_specs=[spec, spec],
        out_shape=[
            jax.ShapeDtypeStruct((10, 2, 128, 128), F32),
            jax.ShapeDtypeStruct((2, 320, 128), F32),
        ],
        scratch_shapes=[
            VMEM((2, 2, 512, 128), F32),
            VMEM((512, 512), BF16),
            VMEM((512, 512), BF16),
            VMEM((256, 1024), BF16),
            VMEM((256, 1024), BF16),
            VMEM((512, 1024), BF16),
            VMEM((512, 1024), BF16),
        ],
        compiler_params=pltpu.CompilerParams(vmem_limit_bytes=40 << 20),
        cost_estimate=pl.CostEstimate(flops=4000000000, bytes_accessed=4000000, transcendentals=0),
        name="correlator",
    )(recv)


def starts_kernel(target, out):
    digit = lax.broadcasted_iota(I32, (32, 128), 0)
    total = jnp.zeros((32, 32), F32)
    for block in range(40):
        high_parts = []
        low_parts = []
        for j in range(8):
            row = target[block * 8 + j : block * 8 + j + 1, :]
            high_parts.append((digit == (row >> 5)).astype(F32).astype(BF16))
            low_parts.append((digit == (row & 31)).astype(F32).astype(BF16))
        total = total + dot_nt(jnp.concatenate(high_parts, 1), jnp.concatenate(low_parts, 1))
    row = lax.broadcasted_iota(I32, (32, 32), 0)
    col = lax.broadcasted_iota(I32, (32, 32), 1)
    below = (col < row).astype(F32).astype(BF16)
    above = (row < col).astype(F32).astype(BF16)
    counts = total.astype(BF16)
    rows_before = lax.dot_general(below, counts, NN, preferred_element_type=F32)
    within = lax.dot_general(counts, above, NN, preferred_element_type=F32)
    start = jnp.sum(rows_before, axis=1, keepdims=True) + within
    start = jnp.minimum(start, 40959.0)
    line = jnp.floor((start + 0.5) * (1.0 / 320.0))
    place = start - line * 320.0
    code = total * 65536.0 + line * 512.0 + place
    out[...] = code.astype(I32)


def record_starts(target):
    spec = pl.BlockSpec(memory_space=VMEM)
    return pl.pallas_call(
        starts_kernel,
        in_specs=[spec],
        out_specs=spec,
        out_shape=jax.ShapeDtypeStruct((32, 32), I32),
        cost_estimate=pl.CostEstimate(flops=100000000, bytes_accessed=200000, transcendentals=0),
        name="record_starts",
    )(target)


def merge_pairs(low, count, step):
    jump = step * 2
    if jump >= count:
        return [(low, low + step)]
    inner = merge_pairs(low, count, jump) + merge_pairs(low + step, count, jump)
    return inner + [(i, i + step) for i in range(low + step, low + count - step, jump)]


def sort_pairs(low, count):
    if count == 1:
        return []
    half = count // 2
    return sort_pairs(low, half) + sort_pairs(low + half, half) + merge_pairs(low, count, 1)


def column_merges():
    pairs = []
    for low, count in ((0, 16), (16, 16), (0, 32), (0, 64)):
        pairs += merge_pairs(low, count, 1)
    return [(a, b) for a, b in pairs if b < 40]


SORT_EIGHT = sort_pairs(0, 8)
SORT_FIVE = [(0, 1), (3, 4), (2, 4), (2, 3), (0, 3), (0, 2), (1, 4), (1, 3), (1, 2)]


def column_steps():
    held = list(range(10))
    pair = "pair"
    phases = []
    for phase in range(1, 11):
        direction = held.index(phase) if phase < 10 else None
        before = held.index(phase - 1)
        steps = []
        for bit in range(phase - 1, -1, -1):
            place = held.index(bit)
            pair, held[place] = held[place], pair
            steps.append((place, True))
        place = held.index("pair")
        pair, held[place] = held[place], pair
        steps.append((place, False))
        phases.append((before, direction, steps))
    steps = []
    for first in range(10):
        if held[first] == first:
            continue
        place = first
        while True:
            pair, held[place] = held[place], pair
            steps.append((place, False))
            if pair == "pair":
                break
            place = pair
    phases[-1] = (phases[-1][0], phases[-1][1], phases[-1][2] + steps)
    return phases


def exchange(low, high):
    swap = low[0] > high[0]
    first = [jnp.where(swap, b, a) for a, b in zip(low, high)]
    second = [jnp.where(swap, a, b) for a, b in zip(low, high)]
    return first, second


def run_pairs(rows, pairs):
    for a, b in pairs:
        rows[a], rows[b] = exchange(rows[a], rows[b])
    return rows


def window_kernel(picks, masked, *args):
    n = len(picks)
    files = args[:-6]
    target, starts, out, key, data, zext = args[-6:]
    sub = lax.broadcasted_iota(I32, (8, 128), 0)
    lan = lax.broadcasted_iota(I32, (8, 128), 1)

    def bit_of(place):
        return (sub >> place) & 1 if place < 3 else (lan >> (place - 3)) & 1

    def rows_of(v):
        if isinstance(v, int):
            return slice(v * 8, v * 8 + 8)
        return pl.ds(pl.multiple_of(v * 8, 8), 8)

    def load(v):
        return [key[rows_of(v), :]] + [data[f, rows_of(v), :] for f in range(n)]

    def store(v, values):
        key[rows_of(v), :] = values[0]
        for f in range(n):
            data[f, rows_of(v), :] = values[1 + f]

    first_flip = -bit_of(0)

    def sort_eight(g, carry):
        rows = []
        for i in range(8):
            v = g * 8 + i
            number = v * 1024 + sub * 128 + lan
            row = [((target[rows_of(v), :] << 16) | number) ^ first_flip]
            rows.append(row + [files[ref][index, rows_of(v), :] for ref, index in picks])
        rows = run_pairs(rows, SORT_EIGHT)
        for i in range(8):
            store(g * 8 + i, rows[i])
        return carry

    lax.fori_loop(0, 5, sort_eight, 0)
    for a, b in column_merges():
        low, high = exchange(load(a), load(b))
        store(a, low)
        store(b, high)

    for before, direction, steps in column_steps():
        change = -bit_of(before)
        if direction is not None:
            change = change ^ -bit_of(direction)

        def across(g, carry):
            pairs = []
            for i in range(4):
                a, b = load(g * 4 + i), load(20 + g * 4 + i)
                a[0] = a[0] ^ change
                b[0] = b[0] ^ change
                pairs.append((a, b))
            for place, compare in steps:
                is_low = bit_of(place) == 0
                axis, size, bit = (0, 8, place) if place < 3 else (1, 128, place - 3)
                near, far = 1 << bit, size - (1 << bit)
                moved = []
                for a, b in pairs:
                    low = [jnp.where(is_low, x, pltpu.roll(y, near, axis)) for x, y in zip(a, b)]
                    high = [jnp.where(is_low, pltpu.roll(x, far, axis), y) for x, y in zip(a, b)]
                    moved.append(exchange(low, high) if compare else (low, high))
                pairs = moved
            for i in range(4):
                store(g * 4 + i, pairs[i][0])
                store(20 + g * 4 + i, pairs[i][1])
            return carry

        def wide(i, carry):
            rows = [load(i + 10 * j) for j in range(4)]
            rows = run_pairs(rows, [(0, 2), (1, 3), (0, 1), (2, 3)])
            for j in range(4):
                store(i + 10 * j, rows[j])
            return carry

        def narrow(g, carry):
            rows = [load(g * 10 + j) for j in range(10)]
            rows = run_pairs(rows, [(j, j + 5) for j in range(5)])
            rows = run_pairs(rows[:5], SORT_FIVE) + run_pairs(rows[5:], SORT_FIVE)
            for j in range(10):
                store(g * 10 + j, rows[j])
            return carry

        lax.fori_loop(0, 5, across, 0)
        lax.fori_loop(0, 10, wide, 0)
        lax.fori_loop(0, 4, narrow, 0)

    for f in range(n):
        line = jnp.concatenate([data[f, pl.ds(s, 40, stride=8), :] for s in range(8)], 0)
        after = pltpu.roll(line[:128], 127, 1)
        padded = jnp.concatenate([line, after, after[:64]], 0)
        for t in range(4):
            zext[t, pl.ds(f, 128, stride=8), :] = padded[t * 128 : (t + 1) * 128].T

    def windows(d, carry):
        tiles = [None] * 5
        for k in range(8):
            code = starts[d >> 2, (d & 3) * 8 + k]
            count, line, place = code >> 16, (code >> 9) & 127, code & 511
            tile, shift = place >> 7, place & 127
            rows = pl.ds(pl.multiple_of(line * 8, 8), 8)
            joined = jnp.where(lan >= shift, zext[tile, rows, :], zext[tile + 1, rows, :])
            index, offset = (80 * k) // 128, (80 * k) % 128
            value = pltpu.roll(joined, (offset - shift) & 127, 1)
            if masked:
                value = jnp.where(((lan - offset) & 127) < count, value, 0.0)
            tiles[index] = jnp.where(lan >= offset, value, tiles[index]) if offset else value
            if offset + 80 > 128:
                tiles[index + 1] = value
        for t in range(5):
            out[pl.ds(d * (5 * n) + t * n, n), :] = tiles[t][:n]
        return carry

    lax.fori_loop(0, 128, windows, 0)


def sort_to_windows(files, picks, target, starts, masked, name):
    n = len(picks)
    spec = pl.BlockSpec(memory_space=VMEM)
    return pl.pallas_call(
        functools.partial(window_kernel, picks, masked),
        in_specs=[spec] * (len(files) + 1) + [pl.BlockSpec(memory_space=SMEM)],
        out_specs=spec,
        out_shape=jax.ShapeDtypeStruct((640 * n, 128), F32),
        scratch_shapes=[
            VMEM((320, 128), I32),
            VMEM((n, 320, 128), F32),
            VMEM((4, 1024, 128), F32),
        ],
        compiler_params=pltpu.CompilerParams(vmem_limit_bytes=32 << 20),
        cost_estimate=pl.CostEstimate(flops=200000000, bytes_accessed=3000000 * n, transcendentals=0),
        name=name,
    )(*files, target, starts)


def fit_terms():
    nodes = np.cos((np.arange(64) + 0.5) * np.pi / 64)
    square = (nodes + 1) * 0.125
    root = np.sqrt(square)
    cheb = np.polynomial.chebyshev
    sine = cheb.cheb2poly(cheb.chebfit(nodes, np.sin(np.pi * root) / root, 5))
    cosine = cheb.cheb2poly(cheb.chebfit(nodes, np.cos(np.pi * root), 5))

    def shifted(poly):
        total = np.zeros(1)
        for term in poly[::-1]:
            total = np.polynomial.polynomial.polyadd(
                np.polynomial.polynomial.polymul(total, [-1.0, 8.0]), [term]
            )
        return [float(x) for x in total[:6]]

    return shifted(sine), shifted(cosine)


SINE, COSINE = fit_terms()
ROUNDER = 12582912.0


def cos_sin_turns(turns):
    r = turns - ((turns + ROUNDER) - ROUNDER)
    square = r * r
    s = jnp.full_like(square, SINE[5])
    c = jnp.full_like(square, COSINE[5])
    for i in range(4, -1, -1):
        s = s * square + SINE[i]
        c = c * square + COSINE[i]
    s = s * r
    twice = s + s
    return 1.0 - twice * s, twice * c


def mixing():
    mix = np.zeros((64, 64), np.float32)
    for k in range(16):
        for sign, row in ((1.0, 16 + k), (-1.0, 15 - k)):
            mix[row, k] = 1.0
            mix[row, 48 + k] = -sign
            mix[32 + row, 16 + k] = 1.0
            mix[32 + row, 32 + k] = sign
    return mix


CHUNK = 20


def grid_kernel(uvw, values, mix, out, table, left, right):
    for t in range(5):
        rows = slice(t * 128, (t + 1) * 128)
        for f in range(3):
            table[f, rows, :] = uvw[pl.ds(t * 3 + f, 128, stride=15), :].T
        for f in range(2):
            table[3 + f, rows, :] = values[pl.ds(t * 2 + f, 128, stride=10), :].T
    line = lax.broadcasted_iota(I32, (8, 128), 0).astype(F32)
    low = (line + 0.5) * (1.0 / 32.0)
    high = (line + 8.5) * (1.0 / 32.0)
    low_w = low * low * -0.5
    high_w = high * high * -0.5

    def turned(c, s, x, y):
        return c * x - s * y, s * x + c * y

    def rows16(a, b):
        return jnp.concatenate([a, b], 0)

    def put(ref, block, lanes, parts):
        for i, part in enumerate(parts):
            top, bottom = split_bf16(part)
            ref[block, i * 16 : i * 16 + 16, lanes] = top
            ref[block, 64 + i * 16 : 80 + i * 16, lanes] = bottom

    def one_subgrid(k, carry):
        total = jnp.zeros((128, 128), F32)
        for block in range(80 // CHUNK):
            for i in range(CHUNK):
                row = k * 80 + block * CHUNK + i
                u, v, w, re, im = [table[f, pl.ds(row, 1), :] for f in range(5)]
                lanes = slice(i * 128, (i + 1) * 128)
                cu, su = cos_sin_turns(low * u)
                cv, sv = cos_sin_turns(low * v)
                step_cu, step_su = cos_sin_turns(u * 0.25)
                step_cv, step_sv = cos_sin_turns(v * 0.25)
                cu2, su2 = turned(cu, su, step_cu, step_su)
                cv2, sv2 = turned(cv, sv, step_cv, step_sv)
                cw, sw = cos_sin_turns(low_w * w)
                cw2, sw2 = cos_sin_turns(high_w * w)
                xr, xi = turned(cw, sw, re, im)
                xr2, xi2 = turned(cw2, sw2, re, im)
                put(
                    left,
                    block,
                    lanes,
                    [
                        rows16(xr * cu, xr2 * cu2),
                        rows16(xi * cu, xi2 * cu2),
                        rows16(xr * su, xr2 * su2),
                        rows16(xi * su, xi2 * su2),
                    ],
                )
                put(
                    right,
                    block,
                    lanes,
                    [
                        rows16(cw * cv, cw2 * cv2),
                        rows16(sw * cv, sw2 * cv2),
                        rows16(cw * sv, cw2 * sv2),
                        rows16(sw * sv, sw2 * sv2),
                    ],
                )
            total = total + dot_nt(left[block], right[block])
        product = (total[:64, :64] + total[64:, 64:]) + (total[:64, 64:] + total[64:, :64])
        exact = functools.partial(
            lax.dot_general, precision=lax.Precision.HIGHEST, preferred_element_type=F32
        )
        grid = exact(exact(mix[...], product, NN), mix[...], NT)
        out[k, 0] = grid[:32, :32] - grid[32:, 32:]
        out[k, 1] = grid[:32, 32:] + grid[32:, :32]
        return carry

    lax.fori_loop(0, 8, one_subgrid, 0)


def grid_records(uvw, values):
    spec = pl.BlockSpec(memory_space=VMEM)
    lanes = CHUNK * 128
    return pl.pallas_call(
        grid_kernel,
        in_specs=[spec, spec, spec],
        out_specs=spec,
        out_shape=jax.ShapeDtypeStruct((8, 2, 32, 32), F32),
        scratch_shapes=[
            VMEM((5, 640, 128), F32),
            VMEM((80 // CHUNK, 128, lanes), BF16),
            VMEM((80 // CHUNK, 128, lanes), BF16),
        ],
        compiler_params=pltpu.CompilerParams(vmem_limit_bytes=40 << 20),
        cost_estimate=pl.CostEstimate(flops=3000000000, bytes_accessed=5000000, transcendentals=0),
        name="gridding",
    )(uvw, values, jnp.asarray(mixing()))


def to_owners(block):
    rows = block.shape[0] // 128
    moved = lax.all_to_all(
        block.reshape(128, 1, rows * 128), AXES, split_axis=0, concat_axis=0, tiled=True
    )
    return moved.reshape(128 * rows, 128)


def per_device(voltages, prototype, uv_cells, w_cells, subgrid_of):
    tail = voltages[:, :, 29:, :].transpose(0, 2, 1, 3)
    count = lax.axis_size("img")
    earlier = lax.ppermute(tail, "img", [(i, i + 1) for i in range(count - 1)])
    spectra = to_owners(channelize(voltages, earlier, prototype))

    target = subgrid_of.reshape(320, 128)
    starts = record_starts(target)
    places = [uv_cells.reshape(2, 320, 128), w_cells.reshape(1, 320, 128)]
    uvw = sort_to_windows(
        places, ((0, 0), (0, 1), (1, 0)), target, starts, False, "sort_places"
    )
    uvw = to_owners(uvw)

    visibilities, stokes = correlate(spectra)
    values = sort_to_windows(
        [stokes], ((0, 0), (0, 1)), target, starts, True, "sort_values"
    )
    values = to_owners(values)
    grids = grid_records(uvw, values)
    return visibilities[None], grids.reshape(8, 2, 1024)


def solution(mesh):
    placed = (
        P(None, "stn", "img", None),
        P(),
        P(None, ("stn", "img")),
        P(("stn", "img")),
        P(("stn", "img"), None),
    )
    return jax.shard_map(
        per_device,
        mesh=mesh,
        in_specs=placed,
        out_specs=(P(("stn", "img"), None, None, None, None), P(("stn", "img"), None, None)),
        check_vma=False,
    )
```

time: 1270 us -> 185 us (0.15)
  local copies, waits for them, and re-layouts: 762 us -> 7.43 us
  other arithmetic: 394 us -> 0 us
  Pallas kernels: 0 us -> 122 us
  waiting for transfers between devices: 55 us -> 3.65 us
  matrix products: 29.9 us -> 0 us
  blocking collectives: 0 us -> 24.5 us
    gather x2 -> x0, local copies, waits for them, and re-layouts: 388 us -> none  [the longest x1 226 us: pack_records(): ranked = targets[order]]
    scatter-add x1 -> x0, other arithmetic: 283 us -> none  [pack_records(): jax.ops.segment_sum(jnp.ones_like(targets), targets, num_segments=nsub)]
    scatter x2 -> x0, local copies, waits for them, and re-layouts: 267 us -> none  [the longest x1 150 us: pack_records(): slots = jnp.zeros((total,), jnp.int32).at[order].set(ranked * most + within)]
    pallas_call x0 -> x6, Pallas kernels: none -> 122 us  [the longest x2 70.5 us: sort_to_windows(): pl.pallas_call(functools.partial(window_kernel, picks, masked), in_specs=...]
    cos x8 -> x0, other arithmetic: 76.8 us -> none  [phase_table(): return (jnp.cos(angle), jnp.sin(angle))]
    all_to_all x2, waiting for transfers between devices: 54.9 us -> 0.01 us  [to_owners(): lax.all_to_all(block.reshape(128, 1, rows * 128), AXES, split_axis=0, con...]
    slice x17 -> x1, local copies, waits for them, and re-layouts: 35.5 us -> 1.22 us  [per_device(): tail = voltages[:, :, 29:, :].transpose(0, 2, 1, 3)]
    dot_general x13 -> x0, matrix products: 29.9 us -> none  [the longest x8 17.7 us: grid_one(): lax.dot_general(left_side, right_side, (((1,), (1,)), ((), ())), precisio...]
  transfers between devices with their start and end apart: 3 -> 3, of which waited for: 2 -> 1; matrix products, arithmetic and copies ran while one was open for 67% -> 0% of each run, Pallas kernels for 0% -> 43%
where the time goes in v1:
time: 185 us; the launch traced here: 184 us
  Pallas kernels  122 us (66%)
  starting transfers between devices  25.7 us (14%)
  blocking collectives  24.5 us (13%)
  local copies, waits for them, and re-layouts  7.43 us (4%)
  waiting for transfers between devices  3.65 us (2%)
    pallas_call x2, Pallas kernels, sort_to_windows(): pl.pallas_call(functools.partial(window_kernel, picks, masked), in_specs=...  70.5 us
    pallas_call x1, Pallas kernels, grid_records(): pl.pallas_call(grid_kernel, in_specs=[spec, spec, spec], out_specs=spec,...  38.2 us
    all_to_all x1, blocking collectives, to_owners(): lax.all_to_all(block.reshape(128, 1, rows * 128), AXES, split_axis=0, con...  24.5 us
    all_to_all x2, starting transfers between devices, to_owners(): lax.all_to_all(block.reshape(128, 1, rows * 128), AXES, split_axis=0, con...  21.1 us
    pallas_call x1, Pallas kernels, correlate(): pl.pallas_call(correlate_kernel, in_specs=[spec], out_specs=[spec, spec],...  5.72 us
    pallas_call x1, Pallas kernels, channelize(): pl.pallas_call(channel_kernel, grid=(4,), in_specs=[pl.BlockSpec((2, 8, 3...  5.49 us
    unnamed x22, local copies, waits for them, and re-layouts  5.36 us
    ppermute x1, starting transfers between devices, per_device(): earlier = lax.ppermute(tail, 'img', [(i, i + 1) for i in range(count - 1)])  4.59 us
  transfers between devices with their start and end apart: 3, of which 1 were waited for; matrix products, arithmetic and copies ran while one was open for 0% of the time, Pallas kernels for 43%

profile of v1, /device:TPU:1, one launch (start us, length us, event | category | flops | bytes accessed | tf_op | source)
XLA Modules:
  0.0 184.4 jit_solution(6977149233654491671)
XLA Ops:
  0.6 1.2 slice.3
  1.9 4.6 %collective-permute-start = (f32[2,3,32,384]{3,2,1,0:T(8,128)S(1)}, f32[2,3,32,384]{3,2,1,0:T(8,128)S(1)}, u32[]{:S(2)}, u32[]{:S(2)}) collective-permute-start(f32[2,3,32,384]{3,2,1,0:T(8,128)S(1)} %bitcast.28), channel_id=1, source_target_pairs={{0,1},{1,2},{2,3},{3,4},{4,5},{5,6},{6,7},{8,9},{9,10},{10,11},{11... | collective-permute-start | bytes 884744 | tf_op jit(solution)/shard_map/ppermute | solution.py:613
  6.5 3.6 %collective-permute-done.halo = f32[2,3,32,384]{3,2,1,0:T(8,128)S(1)} collective-permute-done((f32[2,3,32,384]{3,2,1,0:T(8,128)S(1)}, f32[2,3,32,384]{3,2,1,0:T(8,128)S(1)}, u32[]{:S(2)}, u32[]{:S(2)}) %collective-permute-start) | collective-permute-done | bytes 294944 | tf_op jit(solution)/shard_map/ppermute | solution.py:613
  10.1 1.9 %copy-done = f32[2,32,32,384]{3,2,1,0:T(8,128)S(1)} copy-done((f32[2,32,32,384]{3,2,1,0:T(8,128)S(1)}, f32[2,32,32,384]{3,2,1,0:T(8,128)}, u32[]{:S(2)}) %copy-start) | copy-done | bytes 3145752
  12.0 1.0 copy-done.2
  13.0 1.0 copy-done.3
  14.0 0.7 copy-done.7
  14.7 5.5 %channelizer.1 = f32[2048,128]{1,0:T(8,128)} custom-call(f32[2,32,32,384]{3,2,1,0:T(8,128)S(1)} %copy-done, f32[2,3,32,384]{3,2,1,0:T(8,128)S(1)} %collective-permute-done.halo, f32[4,384]{1,0:T(4,128)S(1)} %copy-done.7, bf16[256,768]{1,0:T(8,128)(2,1)S(1)} %copy-done.2, bf16[256,768]{1,0:T(8,128)(2,1)S(1)} %copy-done.3), custom_call_target="tpu_custom_call" | custom-call | flops 1200000000 | bytes 6000000 | tf_op jit(solution)/shard_map/channelizer/pallas_call | solution.py:83
  20.2 11.3 %all-to-all-start = ((f32[128,1,2048]{2,1,0:T(1,128)}), f32[128,1,2048]{2,1,0:T(1,128)S(1)}, u32[]{:S(2)}, u32[]{:S(2)}) async-start(f32[128,1,2048]{2,1,0:T(1,128)} %bitcast.1), calls=%async_computation | async-start | bytes 2097152 | tf_op jit(solution)/shard_map/all_to_all | solution.py:604
  31.5 0.0 copy-done.9
  31.5 2.6 %record_starts.1.args_3_.args_2_ = s32[32,32]{1,0:T(8,128)} custom-call(s32[320,128]{1,0:T(8,128)} %bitcast.22), custom_call_target="tpu_custom_call" | custom-call | flops 100000000 | bytes 200000 | tf_op jit(solution)/shard_map/record_starts/pallas_call | solution.py:239
  34.1 0.0 copy-done.1
  34.1 0.7 copy-done.5
  34.9 36.0 %sort_places.1 = f32[1920,128]{1,0:T(8,128)} custom-call(f32[2,320,128]{2,1,0:T(8,128)S(1)} %bitcast.19, f32[1,320,128]{2,1,0:T(8,128)S(1)} %bitcast.26, s32[320,128]{1,0:T(8,128)S(1)} %bitcast.23, s32[32,32]{1,0:T(8,128)S(1)} %copy-done.5), custom_call_target="tpu_custom_call" | custom-call | flops 200000000 | bytes 9000000 | tf_op jit(solution)/shard_map/sort_places/pallas_call | solution.py:440
  70.9 0.0 all-to-all-done
  70.9 9.8 %all-to-all-start.1 = ((f32[128,1,1920]{2,1,0:T(1,128)}), f32[128,1,1920]{2,1,0:T(1,128)S(1)}, u32[]{:S(2)}, u32[]{:S(2)}) async-start(f32[128,1,1920]{2,1,0:T(1,128)} %bitcast.6), calls=%async_computation.1 | async-start | bytes 1966080 | tf_op jit(solution)/shard_map/all_to_all | solution.py:604
  80.7 0.0 copy-start.6
  80.7 0.0 copy-start.8
  80.7 5.7 %correlator.1 = (f32[10,2,128,128]{3,2,1,0:T(8,128)}, f32[2,320,128]{2,1,0:T(8,128)S(1)}) custom-call(f32[2048,128]{1,0:T(8,128)S(1)} %bitcast.20), custom_call_target="tpu_custom_call" | custom-call | flops 4000000000 | bytes 4000000 | tf_op jit(solution)/shard_map/correlator/pallas_call | solution.py:188
  86.4 34.4 %sort_values.1 = f32[1280,128]{1,0:T(8,128)S(1)} custom-call(f32[2,320,128]{2,1,0:T(8,128)S(1)} %get-tuple-element.5.args_0_, s32[320,128]{1,0:T(8,128)S(1)} %bitcast.24, s32[32,32]{1,0:T(8,128)S(1)} %copy-done.6), custom_call_target="tpu_custom_call" | custom-call | flops 200000000 | bytes 6000000 | tf_op jit(solution)/shard_map/sort_values/pallas_call | solution.py:440
  120.9 0.0 all-to-all-done.1
  120.9 24.5 %all_to_all.15 = f32[128,1,1280]{2,1,0:T(1,128)S(1)} all-to-all(f32[128,1,1280]{2,1,0:T(1,128)S(1)} %bitcast.18), channel_id=1, replica_groups=mesh['stn'=16,'img'=8] {'stn','img'}, dimensions={0} | all-to-all | bytes 1310720 | tf_op jit(solution)/shard_map/all_to_all | solution.py:604
  145.3 38.2 %gridding.1 = f32[8,2,32,32]{3,2,1,0:T(8,128)S(1)} custom-call(f32[1920,128]{1,0:T(8,128)S(1)} %bitcast.21, f32[1280,128]{1,0:T(8,128)S(1)} %bitcast.25, f32[64,64]{1,0:T(8,128)S(1)} %copy-done.8), custom_call_target="tpu_custom_call" | custom-call | flops 3000000000 | bytes 5000000 | tf_op jit(solution)/shard_map/gridding/pallas_call | solution.py:586
  183.5 0.8 reshape.43
  (13 shorter events, 0.1 us)
Async XLA Ops:
  1.9 8.2 %collective-permute-start = (f32[2,3,32,384]{3,2,1,0:T(8,128)S(1)}, f32[2,3,32,384]{3,2,1,0:T(8,128)S(1)}, u32[]{:S(2)}, u32[]{:S(2)}) collective-permute-start(f32[2,3,32,384]{3,2,1,0:T(8,128)S(1)} %bitcast.28), channel_id=1, source_target_pairs={{0,1},{1,2},{2,3},{3,4},{4,5},{5,6},{6,7},{8,9},{9,10},{10,11},{11... | collective-permute-start | bytes 884744 | tf_op jit(solution)/shard_map/ppermute | solution.py:613
  10.1 1.9 %copy-start = (f32[2,32,32,384]{3,2,1,0:T(8,128)S(1)}, f32[2,32,32,384]{3,2,1,0:T(8,128)}, u32[]{:S(2)}) copy-start(f32[2,32,32,384]{3,2,1,0:T(8,128)} %volt.1) | copy-start | bytes 9437188
  12.0 1.0 copy-start.2
  13.0 1.0 copy-start.3
  14.0 0.7 copy-start.7
  14.7 16.8 %copy-start.9 = (f32[2,40960]{1,0:T(2,128)S(1)}, f32[2,40960]{1,0:T(2,128)}, u32[]{:S(2)}) copy-start(f32[2,40960]{1,0:T(2,128)} %param.10) | copy-start | bytes 983044
  14.7 19.4 %copy-start.1 = (s32[40960,1]{0,1:T(1,128)S(1)}, s32[40960,1]{0,1:T(1,128)}, u32[]{:S(2)}) copy-start(s32[40960,1]{0,1:T(1,128)} %param.12) | copy-start | bytes 491524
  14.7 19.4 %copy-start.4 = (f32[40960]{0:T(1024)S(1)}, f32[40960]{0:T(1024)}, u32[]{:S(2)}) copy-start(f32[40960]{0:T(1024)} %param.11) | copy-start | bytes 491524
  20.2 50.7 %all-to-all-start = ((f32[128,1,2048]{2,1,0:T(1,128)}), f32[128,1,2048]{2,1,0:T(1,128)S(1)}, u32[]{:S(2)}, u32[]{:S(2)}) async-start(f32[128,1,2048]{2,1,0:T(1,128)} %bitcast.1), calls=%async_computation | async-start | bytes 2097152 | tf_op jit(solution)/shard_map/all_to_all | solution.py:604
  34.1 0.7 copy-start.5
  70.9 50.0 %all-to-all-start.1 = ((f32[128,1,1920]{2,1,0:T(1,128)}), f32[128,1,1920]{2,1,0:T(1,128)S(1)}, u32[]{:S(2)}, u32[]{:S(2)}) async-start(f32[128,1,1920]{2,1,0:T(1,128)} %bitcast.6), calls=%async_computation.1 | async-start | bytes 1966080 | tf_op jit(solution)/shard_map/all_to_all | solution.py:604
  80.7 5.8 %copy-start.6 = (s32[32,32]{1,0:T(8,128)S(1)}, s32[32,32]{1,0:T(8,128)}, u32[]{:S(2)}) copy-start(s32[32,32]{1,0:T(8,128)} %record_starts.1.args_3_.args_2_) | copy-start | bytes 12292
  80.7 64.6 %copy-start.8 = (f32[64,64]{1,0:T(8,128)S(1)}, f32[64,64]{1,0:T(8,128)}, u32[]{:S(2)}) copy-start(f32[64,64]{1,0:T(8,128)} %constant.8.clone.mix) | copy-start | bytes 49156

commit v2 on v1

--- a/solution.py
+++ b/solution.py
@@ -246,61 +246,7 @@
     )(target)
 
 
-def merge_pairs(low, count, step):
-    jump = step * 2
-    if jump >= count:
-        return [(low, low + step)]
-    inner = merge_pairs(low, count, jump) + merge_pairs(low + step, count, jump)
-    return inner + [(i, i + step) for i in range(low + step, low + count - step, jump)]
-
-
-def sort_pairs(low, count):
-    if count == 1:
-        return []
-    half = count // 2
-    return sort_pairs(low, half) + sort_pairs(low + half, half) + merge_pairs(low, count, 1)
-
-
-def column_merges():
-    pairs = []
-    for low, count in ((0, 16), (16, 16), (0, 32), (0, 64)):
-        pairs += merge_pairs(low, count, 1)
-    return [(a, b) for a, b in pairs if b < 40]
-
-
-SORT_EIGHT = sort_pairs(0, 8)
-SORT_FIVE = [(0, 1), (3, 4), (2, 4), (2, 3), (0, 3), (0, 2), (1, 4), (1, 3), (1, 2)]
-
-
-def column_steps():
-    held = list(range(10))
-    pair = "pair"
-    phases = []
-    for phase in range(1, 11):
-        direction = held.index(phase) if phase < 10 else None
-        before = held.index(phase - 1)
-        steps = []
-        for bit in range(phase - 1, -1, -1):
-            place = held.index(bit)
-            pair, held[place] = held[place], pair
-            steps.append((place, True))
-        place = held.index("pair")
-        pair, held[place] = held[place], pair
-        steps.append((place, False))
-        phases.append((before, direction, steps))
-    steps = []
-    for first in range(10):
-        if held[first] == first:
-            continue
-        place = first
-        while True:
-            pair, held[place] = held[place], pair
-            steps.append((place, False))
-            if pair == "pair":
-                break
-            place = pair
-    phases[-1] = (phases[-1][0], phases[-1][1], phases[-1][2] + steps)
-    return phases
+SORT_FIVE = ((0, 1), (3, 4), (2, 4), (2, 3), (0, 3), (0, 2), (1, 4), (1, 3), (1, 2))
 
 
 def exchange(low, high):
@@ -311,127 +257,145 @@
 
 
 def run_pairs(rows, pairs):
+    rows = list(rows)
     for a, b in pairs:
         rows[a], rows[b] = exchange(rows[a], rows[b])
     return rows
 
 
+def cleaner(count, bits):
+    return [(i, i | 1 << b) for b in bits for i in range(count) if not i >> b & 1]
+
+
 def window_kernel(picks, masked, *args):
     n = len(picks)
-    files = args[:-6]
-    target, starts, out, key, data, zext = args[-6:]
+    files = args[:-8]
+    target, starts, out, key_s, data_s, key_t, data_t, zext = args[-8:]
     sub = lax.broadcasted_iota(I32, (8, 128), 0)
     lan = lax.broadcasted_iota(I32, (8, 128), 1)
 
-    def bit_of(place):
-        return (sub >> place) & 1 if place < 3 else (lan >> (place - 3)) & 1
-
-    def rows_of(v):
-        if isinstance(v, int):
-            return slice(v * 8, v * 8 + 8)
-        return pl.ds(pl.multiple_of(v * 8, 8), 8)
-
-    def load(v):
-        return [key[rows_of(v), :]] + [data[f, rows_of(v), :] for f in range(n)]
-
-    def store(v, values):
-        key[rows_of(v), :] = values[0]
+    def load(key, data, rows):
+        return [key[rows, :]] + [data[f, rows, :] for f in range(n)]
+
+    def store(key, data, rows, values):
+        key[rows, :] = values[0]
         for f in range(n):
-            data[f, rows_of(v), :] = values[1 + f]
-
-    first_flip = -bit_of(0)
-
-    def sort_eight(g, carry):
-        rows = []
-        for i in range(8):
-            v = g * 8 + i
-            number = v * 1024 + sub * 128 + lan
-            row = [((target[rows_of(v), :] << 16) | number) ^ first_flip]
-            rows.append(row + [files[ref][index, rows_of(v), :] for ref, index in picks])
-        rows = run_pairs(rows, SORT_EIGHT)
-        for i in range(8):
-            store(g * 8 + i, rows[i])
+            data[f, rows, :] = values[1 + f]
+
+    def block(s, v):
+        return slice(s * 40 + v * 8, s * 40 + v * 8 + 8)
+
+    def flip(bit, s):
+        if bit is None or bit > 12:
+            return 0
+        if bit < 3:
+            return -((sub >> bit) & 1)
+        if bit < 6:
+            return -((s >> (bit - 3)) & 1)
+        return -((lan >> (bit - 6)) & 1)
+
+    def sort_fives(phase, first):
+        for s in range(8):
+            rows = []
+            for v in range(5):
+                if first:
+                    number = (s * 40 + v * 8) * 128 + sub * 128 + lan
+                    row = [((target[block(s, v), :] << 16) | number) ^ flip(0, s)]
+                    row += [files[ref][index, block(s, v), :] for ref, index in picks]
+                else:
+                    row = load(key_s, data_s, block(s, v))
+                rows.append(row)
+            rows = run_pairs(rows, SORT_FIVE)
+            change = flip(phase, s) ^ flip(phase + 1, s)
+            for v in range(5):
+                if phase < 13:
+                    rows[v][0] = rows[v][0] ^ change
+                    store(key_s, data_s, block(s, v), rows[v])
+                else:
+                    for f in range(n):
+                        data_t[f, pl.ds(s * 40 + v, 8, stride=5), :] = rows[v][1 + f]
+
+    sort_fives(0, True)
+    for phase in range(1, 14):
+        s_bits = [b for b in (2, 1, 0) if b + 3 < phase]
+        lane_bits = phase - 6
+        if lane_bits > 0:
+            for t in range(3):
+                vs = (2 * t, 2 * t + 1) if t < 2 else (4, 4)
+                places = [block(s, v) for v in vs for s in range(8)]
+                parts = [load(key_s, data_s, place) for place in places]
+                turned = [jnp.concatenate(group, 0).T for group in zip(*parts)]
+                rows = [[x[i * 8 : i * 8 + 8] for x in turned] for i in range(16)]
+                rows = run_pairs(rows, cleaner(16, range(lane_bits - 4, -1, -1)))
+                for i in range(16):
+                    at = t * 128 + i * 8
+                    store(key_t, data_t, slice(at, at + 8), rows[i])
+            for t in range(3):
+                for half in range(2):
+                    at = t * 128 + half * 64
+                    places = [pl.ds(at + i, 8, stride=8) for i in range(8)]
+                    rows = [load(key_t, data_t, place) for place in places]
+                    rows = run_pairs(rows, cleaner(8, range(min(lane_bits, 3) - 1, -1, -1)))
+                    for i in range(8):
+                        store(key_t, data_t, places[i], rows[i])
+            for t in range(3):
+                whole = load(key_t, data_t, slice(t * 128, t * 128 + 128))
+                turned = [x.T for x in whole]
+                for a, v in enumerate((2 * t, 2 * t + 1) if t < 2 else (4,)):
+                    rows = []
+                    for s in range(8):
+                        at = (a * 8 + s) * 8
+                        rows.append([x[at : at + 8] for x in turned])
+                    rows = run_pairs(rows, cleaner(8, s_bits))
+                    for s in range(8):
+                        store(key_s, data_s, block(s, v), rows[s])
+        elif s_bits:
+            for v in range(5):
+                rows = [load(key_s, data_s, block(s, v)) for s in range(8)]
+                rows = run_pairs(rows, cleaner(8, s_bits))
+                for s in range(8):
+                    store(key_s, data_s, block(s, v), rows[s])
+        for v in range(5):
+            places = [pl.ds(v * 8 + i, 8, stride=40) for i in range(8)]
+            rows = [load(key_s, data_s, place) for place in places]
+            rows = run_pairs(rows, cleaner(8, range(min(phase, 3) - 1, -1, -1)))
+            for i in range(8):
+                store(key_s, data_s, places[i], rows[i])
+        sort_fives(phase, False)
+
+    for f in range(n):
+        after = pltpu.roll(data_t[f, 0:128, :], 127, 1)
+        tiles = [
+            data_t[f, 0:128, :],
+            data_t[f, 128:256, :],
+            jnp.concatenate([data_t[f, 256:320, :], after[:64]], 0),
+            jnp.concatenate([after[64:], after[64:]], 0),
+        ]
+        for t in range(4):
+            zext[t, pl.ds(f, 128, stride=8), :] = tiles[t].T
+
+    def windows(step, carry):
+        for near in range(4):
+            d = step * 4 + near
+            tiles = [None] * 5
+            for k in range(8):
+                code = starts[step, near * 8 + k]
+                count, line, place = code >> 16, (code >> 9) & 127, code & 511
+                tile, shift = place >> 7, place & 127
+                rows = pl.ds(pl.multiple_of(line * 8, 8), 8)
+                joined = jnp.where(lan >= shift, zext[tile, rows, :], zext[tile + 1, rows, :])
+                index, offset = (80 * k) // 128, (80 * k) % 128
+                value = pltpu.roll(joined, (offset - shift) & 127, 1)
+                if masked:
+                    value = jnp.where(((lan - offset) & 127) < count, value, 0.0)
+                tiles[index] = jnp.where(lan >= offset, value, tiles[index]) if offset else value
+                if offset + 80 > 128:
+                    tiles[index + 1] = value
+            for t in range(5):
+                out[pl.ds(d * (5 * n) + t * n, n), :] = tiles[t][:n]
         return carry
 
-    lax.fori_loop(0, 5, sort_eight, 0)
-    for a, b in column_merges():
-        low, high = exchange(load(a), load(b))
-        store(a, low)
-        store(b, high)
-
-    for before, direction, steps in column_steps():
-        change = -bit_of(before)
-        if direction is not None:
-            change = change ^ -bit_of(direction)
-
-        def across(g, carry):
-            pairs = []
-            for i in range(4):
-                a, b = load(g * 4 + i), load(20 + g * 4 + i)
-                a[0] = a[0] ^ change
-                b[0] = b[0] ^ change
-                pairs.append((a, b))
-            for place, compare in steps:
-                is_low = bit_of(place) == 0
-                axis, size, bit = (0, 8, place) if place < 3 else (1, 128, place - 3)
-                near, far = 1 << bit, size - (1 << bit)
-                moved = []
-                for a, b in pairs:
-                    low = [jnp.where(is_low, x, pltpu.roll(y, near, axis)) for x, y in zip(a, b)]
-                    high = [jnp.where(is_low, pltpu.roll(x, far, axis), y) for x, y in zip(a, b)]
-                    moved.append(exchange(low, high) if compare else (low, high))
-                pairs = moved
-            for i in range(4):
-                store(g * 4 + i, pairs[i][0])
-                store(20 + g * 4 + i, pairs[i][1])
-            return carry
-
-        def wide(i, carry):
-            rows = [load(i + 10 * j) for j in range(4)]
-            rows = run_pairs(rows, [(0, 2), (1, 3), (0, 1), (2, 3)])
-            for j in range(4):
-                store(i + 10 * j, rows[j])
-            return carry
-
-        def narrow(g, carry):
-            rows = [load(g * 10 + j) for j in range(10)]
-            rows = run_pairs(rows, [(j, j + 5) for j in range(5)])
-            rows = run_pairs(rows[:5], SORT_FIVE) + run_pairs(rows[5:], SORT_FIVE)
-            for j in range(10):
-                store(g * 10 + j, rows[j])
-            return carry
-
-        lax.fori_loop(0, 5, across, 0)
-        lax.fori_loop(0, 10, wide, 0)
-        lax.fori_loop(0, 4, narrow, 0)
-
-    for f in range(n):
-        line = jnp.concatenate([data[f, pl.ds(s, 40, stride=8), :] for s in range(8)], 0)
-        after = pltpu.roll(line[:128], 127, 1)
-        padded = jnp.concatenate([line, after, after[:64]], 0)
-        for t in range(4):
-            zext[t, pl.ds(f, 128, stride=8), :] = padded[t * 128 : (t + 1) * 128].T
-
-    def windows(d, carry):
-        tiles = [None] * 5
-        for k in range(8):
-            code = starts[d >> 2, (d & 3) * 8 + k]
-            count, line, place = code >> 16, (code >> 9) & 127, code & 511
-            tile, shift = place >> 7, place & 127
-            rows = pl.ds(pl.multiple_of(line * 8, 8), 8)
-            joined = jnp.where(lan >= shift, zext[tile, rows, :], zext[tile + 1, rows, :])
-            index, offset = (80 * k) // 128, (80 * k) % 128
-            value = pltpu.roll(joined, (offset - shift) & 127, 1)
-            if masked:
-                value = jnp.where(((lan - offset) & 127) < count, value, 0.0)
-            tiles[index] = jnp.where(lan >= offset, value, tiles[index]) if offset else value
-            if offset + 80 > 128:
-                tiles[index + 1] = value
-        for t in range(5):
-            out[pl.ds(d * (5 * n) + t * n, n), :] = tiles[t][:n]
-        return carry
-
-    lax.fori_loop(0, 128, windows, 0)
+    lax.fori_loop(0, 32, windows, 0)
 
 
 def sort_to_windows(files, picks, target, starts, masked, name):
@@ -445,6 +409,8 @@
         scratch_shapes=[
             VMEM((320, 128), I32),
             VMEM((n, 320, 128), F32),
+            VMEM((384, 128), I32),
+            VMEM((n, 384, 128), F32),
             VMEM((4, 1024, 128), F32),
         ],
         compiler_params=pltpu.CompilerParams(vmem_limit_bytes=32 << 20),
@@ -476,8 +442,8 @@
 ROUNDER = 12582912.0
 
 
-def cos_sin_turns(turns):
-    r = turns - ((turns + ROUNDER) - ROUNDER)
+def cos_sin_turns(turns, reduce):
+    r = turns - ((turns + ROUNDER) - ROUNDER) if reduce else turns
     square = r * r
     s = jnp.full_like(square, SINE[5])
     c = jnp.full_like(square, COSINE[5])
@@ -500,74 +466,95 @@
     return mix
 
 
-CHUNK = 20
-
-
-def grid_kernel(uvw, values, mix, out, table, left, right):
+CHUNK = 16
+
+
+def turned(c, s, x, y):
+    return c * x - s * y, s * x + c * y
+
+
+def powers(c, s, step_c, step_s, count):
+    out = [(c, s)]
+    for _ in range(count - 1):
+        out.append(turned(*out[-1], step_c, step_s))
+    return out
+
+
+def grid_kernel(uvw, values, mix, out, table, stage, steps, left, right):
     for t in range(5):
         rows = slice(t * 128, (t + 1) * 128)
         for f in range(3):
             table[f, rows, :] = uvw[pl.ds(t * 3 + f, 128, stride=15), :].T
         for f in range(2):
             table[3 + f, rows, :] = values[pl.ds(t * 2 + f, 128, stride=10), :].T
-    line = lax.broadcasted_iota(I32, (8, 128), 0).astype(F32)
-    low = (line + 0.5) * (1.0 / 32.0)
-    high = (line + 8.5) * (1.0 / 32.0)
-    low_w = low * low * -0.5
-    high_w = high * high * -0.5
-
-    def turned(c, s, x, y):
-        return c * x - s * y, s * x + c * y
-
-    def rows16(a, b):
-        return jnp.concatenate([a, b], 0)
-
-    def put(ref, block, lanes, parts):
-        for i, part in enumerate(parts):
-            top, bottom = split_bf16(part)
-            ref[block, i * 16 : i * 16 + 16, lanes] = top
-            ref[block, 64 + i * 16 : 80 + i * 16, lanes] = bottom
+
+    def make_stage(k, block):
+        rows = pl.ds(pl.multiple_of(k * 80 + block * 8, 8), 8)
+        u, v, w = [table[f, rows, :] for f in range(3)]
+        for axis, coord in enumerate((u, v)):
+            c, s = cos_sin_turns(coord * (1.0 / 64.0), False)
+            step = (1.0 - 2.0 * s * s, 2.0 * s * c)
+            for i, (x, y) in enumerate(powers(c, s, *step, 8)):
+                stage[block, (axis * 16 + i) * 8 : (axis * 16 + i) * 8 + 8, :] = x
+                stage[block, (axis * 16 + 8 + i) * 8 : (axis * 16 + 8 + i) * 8 + 8, :] = y
+            for _ in range(3):
+                step = (1.0 - 2.0 * step[1] * step[1], 2.0 * step[1] * step[0])
+            steps[block, axis * 16 : axis * 16 + 8, :] = step[0]
+            steps[block, axis * 16 + 8 : axis * 16 + 16, :] = step[1]
+        first = cos_sin_turns(w * (-1.0 / 8192.0), False)
+        step = cos_sin_turns(w * (-1.0 / 1024.0), False)
+        steps_w = powers(*step, *step, 15)
+        for i in range(16):
+            if i:
+                first = turned(*first, *steps_w[i - 1])
+            stage[block, (32 + i) * 8 : (32 + i) * 8 + 8, :] = first[0]
+            stage[block, (48 + i) * 8 : (48 + i) * 8 + 8, :] = first[1]
+
+    def use_stage(k, block, i):
+        row = pl.ds(k * 80 + block * 8 + i, 1)
+        re, im = table[3, row, :], table[4, row, :]
+
+        def staged(slot):
+            return stage[block, pl.ds(slot * 8 + i, 8, stride=8), :]
+
+        def step_of(slot):
+            return steps[block, slot * 8 + i : slot * 8 + i + 1, :]
+
+        cu, su, cv, sv, cw, cw2, sw, sw2 = [staged(8 * j) for j in range(8)]
+        cu2, su2 = turned(cu, su, step_of(0), step_of(1))
+        cv2, sv2 = turned(cv, sv, step_of(2), step_of(3))
+        xr, xi = turned(cw, sw, re, im)
+        xr2, xi2 = turned(cw2, sw2, re, im)
+        join = lambda a, b: jnp.concatenate([a, b], 0)
+        lefts = [
+            join(xr * cu, xr2 * cu2),
+            join(xi * cu, xi2 * cu2),
+            join(xr * su, xr2 * su2),
+            join(xi * su, xi2 * su2),
+        ]
+        rights = [
+            join(cw * cv, cw2 * cv2),
+            join(sw * cv, sw2 * cv2),
+            join(cw * sv, cw2 * sv2),
+            join(sw * sv, sw2 * sv2),
+        ]
+        chunk, at = divmod(block * 8 + i, CHUNK)
+        lanes = slice(at * 128, at * 128 + 128)
+        for ref, parts in ((left, lefts), (right, rights)):
+            for j, part in enumerate(parts):
+                top, bottom = split_bf16(part)
+                ref[chunk, j * 16 : j * 16 + 16, lanes] = top
+                ref[chunk, 64 + j * 16 : 80 + j * 16, lanes] = bottom
 
     def one_subgrid(k, carry):
         total = jnp.zeros((128, 128), F32)
-        for block in range(80 // CHUNK):
-            for i in range(CHUNK):
-                row = k * 80 + block * CHUNK + i
-                u, v, w, re, im = [table[f, pl.ds(row, 1), :] for f in range(5)]
-                lanes = slice(i * 128, (i + 1) * 128)
-                cu, su = cos_sin_turns(low * u)
-                cv, sv = cos_sin_turns(low * v)
-                step_cu, step_su = cos_sin_turns(u * 0.25)
-                step_cv, step_sv = cos_sin_turns(v * 0.25)
-                cu2, su2 = turned(cu, su, step_cu, step_su)
-                cv2, sv2 = turned(cv, sv, step_cv, step_sv)
-                cw, sw = cos_sin_turns(low_w * w)
-                cw2, sw2 = cos_sin_turns(high_w * w)
-                xr, xi = turned(cw, sw, re, im)
-                xr2, xi2 = turned(cw2, sw2, re, im)
-                put(
-                    left,
-                    block,
-                    lanes,
-                    [
-                        rows16(xr * cu, xr2 * cu2),
-                        rows16(xi * cu, xi2 * cu2),
-                        rows16(xr * su, xr2 * su2),
-                        rows16(xi * su, xi2 * su2),
-                    ],
-                )
-                put(
-                    right,
-                    block,
-                    lanes,
-                    [
-                        rows16(cw * cv, cw2 * cv2),
-                        rows16(sw * cv, sw2 * cv2),
-                        rows16(cw * sv, cw2 * sv2),
-                        rows16(sw * sv, sw2 * sv2),
-                    ],
-                )
-            total = total + dot_nt(left[block], right[block])
+        for block in range(10):
+            make_stage(k, block)
+            for i in range(8):
+                use_stage(k, block, i)
+            if (block + 1) * 8 % CHUNK == 0:
+                chunk = (block + 1) * 8 // CHUNK - 1
+                total = total + dot_nt(left[chunk], right[chunk])
         product = (total[:64, :64] + total[64:, 64:]) + (total[:64, 64:] + total[64:, :64])
         exact = functools.partial(
             lax.dot_general, precision=lax.Precision.HIGHEST, preferred_element_type=F32
@@ -590,6 +577,8 @@
         out_shape=jax.ShapeDtypeStruct((8, 2, 32, 32), F32),
         scratch_shapes=[
             VMEM((5, 640, 128), F32),
+            VMEM((10, 512, 128), F32),
+            VMEM((10, 32, 128), F32),
             VMEM((80 // CHUNK, 128, lanes), BF16),
             VMEM((80 // CHUNK, 128, lanes), BF16),
         ],

time: 185 us -> 135 us (0.73)
  Pallas kernels: 122 us -> 72.1 us
    pallas_call x2, Pallas kernels: 70.5 us -> 28.2 us  [sort_to_windows(): pl.pallas_call(functools.partial(window_kernel, picks, masked), in_specs=...]
    pallas_call x1, Pallas kernels: 38.2 us -> 30 us  [grid_records(): pl.pallas_call(grid_kernel, in_specs=[spec, spec, spec], out_specs=spec,...]
  transfers between devices with their start and end apart: 3 -> 3, of which waited for: 1 -> 2; matrix products, arithmetic and copies ran while one was open for 0% -> 0% of each run, Pallas kernels for 43% -> 27%
where the time goes in v2:
time: 135 us; the launch traced here: 134 us
  Pallas kernels  72.1 us (53%)
  starting transfers between devices  25.2 us (19%)
  blocking collectives  24.5 us (18%)
  local copies, waits for them, and re-layouts  7.43 us (6%)
  waiting for transfers between devices  4.08 us (3%)
    pallas_call x1, Pallas kernels, grid_records(): pl.pallas_call(grid_kernel, in_specs=[spec, spec, spec], out_specs=spec,...  30 us
    pallas_call x2, Pallas kernels, sort_to_windows(): pl.pallas_call(functools.partial(window_kernel, picks, masked), in_specs=...  28.2 us
    all_to_all x1, blocking collectives, to_owners(): lax.all_to_all(block.reshape(128, 1, rows * 128), AXES, split_axis=0, con...  24.5 us
    all_to_all x2, starting transfers between devices, to_owners(): lax.all_to_all(block.reshape(128, 1, rows * 128), AXES, split_axis=0, con...  20.6 us
    pallas_call x1, Pallas kernels, correlate(): pl.pallas_call(correlate_kernel, in_specs=[spec], out_specs=[spec, spec],...  5.72 us
    pallas_call x1, Pallas kernels, channelize(): pl.pallas_call(channel_kernel, grid=(4,), in_specs=[pl.BlockSpec((2, 8, 3...  5.49 us
    unnamed x22, local copies, waits for them, and re-layouts  5.36 us
    ppermute x1, starting transfers between devices, per_device(): earlier = lax.ppermute(tail, 'img', [(i, i + 1) for i in range(count - 1)])  4.59 us
  transfers between devices with their start and end apart: 3, of which 2 were waited for; matrix products, arithmetic and copies ran while one was open for 0% of the time, Pallas kernels for 27%

profile of v2, /device:TPU:1, one launch (start us, length us, event | category | flops | bytes accessed | tf_op | source)
XLA Modules:
  0.0 134.0 jit_solution(10805071775553780891)
XLA Ops:
  0.6 1.2 slice.3
  1.9 4.6 %collective-permute-start = (f32[2,3,32,384]{3,2,1,0:T(8,128)S(1)}, f32[2,3,32,384]{3,2,1,0:T(8,128)S(1)}, u32[]{:S(2)}, u32[]{:S(2)}) collective-permute-start(f32[2,3,32,384]{3,2,1,0:T(8,128)S(1)} %bitcast.28), channel_id=1, source_target_pairs={{0,1},{1,2},{2,3},{3,4},{4,5},{5,6},{6,7},{8,9},{9,10},{10,11},{11... | collective-permute-start | bytes 884744 | tf_op jit(solution)/shard_map/ppermute | solution.py:602
  6.5 3.6 %collective-permute-done.halo = f32[2,3,32,384]{3,2,1,0:T(8,128)S(1)} collective-permute-done((f32[2,3,32,384]{3,2,1,0:T(8,128)S(1)}, f32[2,3,32,384]{3,2,1,0:T(8,128)S(1)}, u32[]{:S(2)}, u32[]{:S(2)}) %collective-permute-start) | collective-permute-done | bytes 294944 | tf_op jit(solution)/shard_map/ppermute | solution.py:602
  10.1 1.9 %copy-done = f32[2,32,32,384]{3,2,1,0:T(8,128)S(1)} copy-done((f32[2,32,32,384]{3,2,1,0:T(8,128)S(1)}, f32[2,32,32,384]{3,2,1,0:T(8,128)}, u32[]{:S(2)}) %copy-start) | copy-done | bytes 3145752
  12.0 1.0 copy-done.2
  13.0 1.0 copy-done.3
  14.0 0.7 copy-done.7
  14.7 5.5 %channelizer.1 = f32[2048,128]{1,0:T(8,128)} custom-call(f32[2,32,32,384]{3,2,1,0:T(8,128)S(1)} %copy-done, f32[2,3,32,384]{3,2,1,0:T(8,128)S(1)} %collective-permute-done.halo, f32[4,384]{1,0:T(4,128)S(1)} %copy-done.7, bf16[256,768]{1,0:T(8,128)(2,1)S(1)} %copy-done.2, bf16[256,768]{1,0:T(8,128)(2,1)S(1)} %copy-done.3), custom_call_target="tpu_custom_call" | custom-call | flops 1200000000 | bytes 6000000 | tf_op jit(solution)/shard_map/channelizer/pallas_call | solution.py:83
  20.2 11.3 %all-to-all-start = ((f32[128,1,2048]{2,1,0:T(1,128)}), f32[128,1,2048]{2,1,0:T(1,128)S(1)}, u32[]{:S(2)}, u32[]{:S(2)}) async-start(f32[128,1,2048]{2,1,0:T(1,128)} %bitcast.1), calls=%async_computation | async-start | bytes 2097152 | tf_op jit(solution)/shard_map/all_to_all | solution.py:593
  31.5 0.0 copy-done.9
  31.5 2.6 %record_starts.1.args_3_.args_2_ = s32[32,32]{1,0:T(8,128)} custom-call(s32[320,128]{1,0:T(8,128)} %bitcast.22), custom_call_target="tpu_custom_call" | custom-call | flops 100000000 | bytes 200000 | tf_op jit(solution)/shard_map/record_starts/pallas_call | solution.py:239
  34.1 0.0 copy-done.1
  34.1 0.7 copy-done.5
  34.9 15.3 %sort_places.1 = f32[1920,128]{1,0:T(8,128)} custom-call(f32[2,320,128]{2,1,0:T(8,128)S(1)} %bitcast.19, f32[1,320,128]{2,1,0:T(8,128)S(1)} %bitcast.26, s32[320,128]{1,0:T(8,128)S(1)} %bitcast.23, s32[32,32]{1,0:T(8,128)S(1)} %copy-done.5), custom_call_target="tpu_custom_call" | custom-call | flops 200000000 | bytes 9000000 | tf_op jit(solution)/shard_map/sort_places/pallas_call | solution.py:404
  50.1 0.4 all-to-all-done
  50.6 9.3 %all-to-all-start.1 = ((f32[128,1,1920]{2,1,0:T(1,128)}), f32[128,1,1920]{2,1,0:T(1,128)S(1)}, u32[]{:S(2)}, u32[]{:S(2)}) async-start(f32[128,1,1920]{2,1,0:T(1,128)} %bitcast.6), calls=%async_computation.1 | async-start | bytes 1966080 | tf_op jit(solution)/shard_map/all_to_all | solution.py:593
  59.9 0.0 copy-start.6
  59.9 0.0 copy-start.8
  59.9 5.7 %correlator.1 = (f32[10,2,128,128]{3,2,1,0:T(8,128)}, f32[2,320,128]{2,1,0:T(8,128)S(1)}) custom-call(f32[2048,128]{1,0:T(8,128)S(1)} %bitcast.20), custom_call_target="tpu_custom_call" | custom-call | flops 4000000000 | bytes 4000000 | tf_op jit(solution)/shard_map/correlator/pallas_call | solution.py:188
  65.7 13.0 %sort_values.1 = f32[1280,128]{1,0:T(8,128)S(1)} custom-call(f32[2,320,128]{2,1,0:T(8,128)S(1)} %get-tuple-element.5.args_0_, s32[320,128]{1,0:T(8,128)S(1)} %bitcast.24, s32[32,32]{1,0:T(8,128)S(1)} %copy-done.6), custom_call_target="tpu_custom_call" | custom-call | flops 200000000 | bytes 6000000 | tf_op jit(solution)/shard_map/sort_values/pallas_call | solution.py:404
  78.6 0.0 all-to-all-done.1
  78.6 24.5 %all_to_all.15 = f32[128,1,1280]{2,1,0:T(1,128)S(1)} all-to-all(f32[128,1,1280]{2,1,0:T(1,128)S(1)} %bitcast.18), channel_id=1, replica_groups=mesh['stn'=16,'img'=8] {'stn','img'}, dimensions={0} | all-to-all | bytes 1310720 | tf_op jit(solution)/shard_map/all_to_all | solution.py:593
  103.1 30.0 %gridding.1 = f32[8,2,32,32]{3,2,1,0:T(8,128)S(1)} custom-call(f32[1920,128]{1,0:T(8,128)S(1)} %bitcast.21, f32[1280,128]{1,0:T(8,128)S(1)} %bitcast.25, f32[64,64]{1,0:T(8,128)S(1)} %copy-done.8), custom_call_target="tpu_custom_call" | custom-call | flops 3000000000 | bytes 5000000 | tf_op jit(solution)/shard_map/gridding/pallas_call | solution.py:573
  133.1 0.8 reshape.43
  (13 shorter events, 0.1 us)
Async XLA Ops:
  1.9 8.2 %collective-permute-start = (f32[2,3,32,384]{3,2,1,0:T(8,128)S(1)}, f32[2,3,32,384]{3,2,1,0:T(8,128)S(1)}, u32[]{:S(2)}, u32[]{:S(2)}) collective-permute-start(f32[2,3,32,384]{3,2,1,0:T(8,128)S(1)} %bitcast.28), channel_id=1, source_target_pairs={{0,1},{1,2},{2,3},{3,4},{4,5},{5,6},{6,7},{8,9},{9,10},{10,11},{11... | collective-permute-start | bytes 884744 | tf_op jit(solution)/shard_map/ppermute | solution.py:602
  10.1 1.9 %copy-start = (f32[2,32,32,384]{3,2,1,0:T(8,128)S(1)}, f32[2,32,32,384]{3,2,1,0:T(8,128)}, u32[]{:S(2)}) copy-start(f32[2,32,32,384]{3,2,1,0:T(8,128)} %volt.1) | copy-start | bytes 9437188
  12.0 1.0 copy-start.2
  13.0 1.0 copy-start.3
  14.0 0.7 copy-start.7
  14.7 16.8 %copy-start.9 = (f32[2,40960]{1,0:T(2,128)S(1)}, f32[2,40960]{1,0:T(2,128)}, u32[]{:S(2)}) copy-start(f32[2,40960]{1,0:T(2,128)} %param.10) | copy-start | bytes 983044
  14.7 19.4 %copy-start.1 = (s32[40960,1]{0,1:T(1,128)S(1)}, s32[40960,1]{0,1:T(1,128)}, u32[]{:S(2)}) copy-start(s32[40960,1]{0,1:T(1,128)} %param.12) | copy-start | bytes 491524
  14.7 19.4 %copy-start.4 = (f32[40960]{0:T(1024)S(1)}, f32[40960]{0:T(1024)}, u32[]{:S(2)}) copy-start(f32[40960]{0:T(1024)} %param.11) | copy-start | bytes 491524
  20.2 30.4 %all-to-all-start = ((f32[128,1,2048]{2,1,0:T(1,128)}), f32[128,1,2048]{2,1,0:T(1,128)S(1)}, u32[]{:S(2)}, u32[]{:S(2)}) async-start(f32[128,1,2048]{2,1,0:T(1,128)} %bitcast.1), calls=%async_computation | async-start | bytes 2097152 | tf_op jit(solution)/shard_map/all_to_all | solution.py:593
  34.1 0.7 copy-start.5
  50.6 28.1 %all-to-all-start.1 = ((f32[128,1,1920]{2,1,0:T(1,128)}), f32[128,1,1920]{2,1,0:T(1,128)S(1)}, u32[]{:S(2)}, u32[]{:S(2)}) async-start(f32[128,1,1920]{2,1,0:T(1,128)} %bitcast.6), calls=%async_computation.1 | async-start | bytes 1966080 | tf_op jit(solution)/shard_map/all_to_all | solution.py:593
  59.9 5.7 %copy-start.6 = (s32[32,32]{1,0:T(8,128)S(1)}, s32[32,32]{1,0:T(8,128)}, u32[]{:S(2)}) copy-start(s32[32,32]{1,0:T(8,128)} %record_starts.1.args_3_.args_2_) | copy-start | bytes 12292
  59.9 43.2 %copy-start.8 = (f32[64,64]{1,0:T(8,128)S(1)}, f32[64,64]{1,0:T(8,128)}, u32[]{:S(2)}) copy-start(f32[64,64]{1,0:T(8,128)} %constant.8.clone.mix) | copy-start | bytes 49156

commit v3 on v2

--- a/solution.py
+++ b/solution.py
@@ -439,11 +439,9 @@
 
 
 SINE, COSINE = fit_terms()
-ROUNDER = 12582912.0
-
-
-def cos_sin_turns(turns, reduce):
-    r = turns - ((turns + ROUNDER) - ROUNDER) if reduce else turns
+
+
+def cos_sin_turns(r):
     square = r * r
     s = jnp.full_like(square, SINE[5])
     c = jnp.full_like(square, COSINE[5])
@@ -466,9 +464,6 @@
     return mix
 
 
-CHUNK = 16
-
-
 def turned(c, s, x, y):
     return c * x - s * y, s * x + c * y
 
@@ -480,112 +475,156 @@
     return out
 
 
-def grid_kernel(uvw, values, mix, out, table, stage, steps, left, right):
+def turn_fields(source, count, table):
     for t in range(5):
         rows = slice(t * 128, (t + 1) * 128)
-        for f in range(3):
-            table[f, rows, :] = uvw[pl.ds(t * 3 + f, 128, stride=15), :].T
-        for f in range(2):
-            table[3 + f, rows, :] = values[pl.ds(t * 2 + f, 128, stride=10), :].T
-
-    def make_stage(k, block):
-        rows = pl.ds(pl.multiple_of(k * 80 + block * 8, 8), 8)
-        u, v, w = [table[f, rows, :] for f in range(3)]
-        for axis, coord in enumerate((u, v)):
-            c, s = cos_sin_turns(coord * (1.0 / 64.0), False)
-            step = (1.0 - 2.0 * s * s, 2.0 * s * c)
-            for i, (x, y) in enumerate(powers(c, s, *step, 8)):
-                stage[block, (axis * 16 + i) * 8 : (axis * 16 + i) * 8 + 8, :] = x
-                stage[block, (axis * 16 + 8 + i) * 8 : (axis * 16 + 8 + i) * 8 + 8, :] = y
-            for _ in range(3):
-                step = (1.0 - 2.0 * step[1] * step[1], 2.0 * step[1] * step[0])
-            steps[block, axis * 16 : axis * 16 + 8, :] = step[0]
-            steps[block, axis * 16 + 8 : axis * 16 + 16, :] = step[1]
-        first = cos_sin_turns(w * (-1.0 / 8192.0), False)
-        step = cos_sin_turns(w * (-1.0 / 1024.0), False)
-        steps_w = powers(*step, *step, 15)
-        for i in range(16):
-            if i:
-                first = turned(*first, *steps_w[i - 1])
-            stage[block, (32 + i) * 8 : (32 + i) * 8 + 8, :] = first[0]
-            stage[block, (48 + i) * 8 : (48 + i) * 8 + 8, :] = first[1]
-
-    def use_stage(k, block, i):
-        row = pl.ds(k * 80 + block * 8 + i, 1)
-        re, im = table[3, row, :], table[4, row, :]
-
-        def staged(slot):
-            return stage[block, pl.ds(slot * 8 + i, 8, stride=8), :]
-
-        def step_of(slot):
-            return steps[block, slot * 8 + i : slot * 8 + i + 1, :]
-
-        cu, su, cv, sv, cw, cw2, sw, sw2 = [staged(8 * j) for j in range(8)]
-        cu2, su2 = turned(cu, su, step_of(0), step_of(1))
-        cv2, sv2 = turned(cv, sv, step_of(2), step_of(3))
-        xr, xi = turned(cw, sw, re, im)
-        xr2, xi2 = turned(cw2, sw2, re, im)
-        join = lambda a, b: jnp.concatenate([a, b], 0)
-        lefts = [
-            join(xr * cu, xr2 * cu2),
-            join(xi * cu, xi2 * cu2),
-            join(xr * su, xr2 * su2),
-            join(xi * su, xi2 * su2),
-        ]
-        rights = [
-            join(cw * cv, cw2 * cv2),
-            join(sw * cv, sw2 * cv2),
-            join(cw * sv, cw2 * sv2),
-            join(sw * sv, sw2 * sv2),
-        ]
-        chunk, at = divmod(block * 8 + i, CHUNK)
-        lanes = slice(at * 128, at * 128 + 128)
-        for ref, parts in ((left, lefts), (right, rights)):
-            for j, part in enumerate(parts):
-                top, bottom = split_bf16(part)
-                ref[chunk, j * 16 : j * 16 + 16, lanes] = top
-                ref[chunk, 64 + j * 16 : 80 + j * 16, lanes] = bottom
-
-    def one_subgrid(k, carry):
-        total = jnp.zeros((128, 128), F32)
-        for block in range(10):
-            make_stage(k, block)
-            for i in range(8):
-                use_stage(k, block, i)
-            if (block + 1) * 8 % CHUNK == 0:
-                chunk = (block + 1) * 8 // CHUNK - 1
-                total = total + dot_nt(left[chunk], right[chunk])
-        product = (total[:64, :64] + total[64:, 64:]) + (total[:64, 64:] + total[64:, :64])
-        exact = functools.partial(
-            lax.dot_general, precision=lax.Precision.HIGHEST, preferred_element_type=F32
-        )
-        grid = exact(exact(mix[...], product, NN), mix[...], NT)
-        out[k, 0] = grid[:32, :32] - grid[32:, 32:]
-        out[k, 1] = grid[:32, 32:] + grid[32:, :32]
-        return carry
-
-    lax.fori_loop(0, 8, one_subgrid, 0)
-
-
-def grid_records(uvw, values):
-    spec = pl.BlockSpec(memory_space=VMEM)
-    lanes = CHUNK * 128
+        for f in range(count):
+            table[f, rows, :] = source[pl.ds(t * count + f, 128, stride=5 * count), :].T
+
+
+def stage_coord(coord, stage, steps, block, base):
+    c, s = cos_sin_turns(coord * (1.0 / 64.0))
+    step = (1.0 - 2.0 * s * s, 2.0 * s * c)
+    for i, (x, y) in enumerate(powers(c, s, *step, 8)):
+        stage[block, (base + i) * 8 : (base + i) * 8 + 8, :] = x
+        stage[block, (base + 8 + i) * 8 : (base + 8 + i) * 8 + 8, :] = y
+    for _ in range(3):
+        step = (1.0 - 2.0 * step[1] * step[1], 2.0 * step[1] * step[0])
+    steps[block, 0:8, :] = step[0]
+    steps[block, 8:16, :] = step[1]
+
+
+def stage_w(w, stage, block, base):
+    first = cos_sin_turns(w * (-1.0 / 8192.0))
+    step = cos_sin_turns(w * (-1.0 / 1024.0))
+    steps_w = powers(*step, *step, 15)
+    for i in range(16):
+        if i:
+            first = turned(*first, *steps_w[i - 1])
+        stage[block, (base + i) * 8 : (base + i) * 8 + 8, :] = first[0]
+        stage[block, (base + 16 + i) * 8 : (base + 16 + i) * 8 + 8, :] = first[1]
+
+
+def staged_row(stage, steps, block, i):
+    low_c, low_s, w_c, w_c2, w_s, w_s2 = [
+        stage[block, pl.ds(j * 64 + i, 8, stride=8), :] for j in range(6)
+    ]
+    step = steps[block, i : i + 1, :], steps[block, 8 + i : 9 + i, :]
+    return low_c, low_s, *turned(low_c, low_s, *step), w_c, w_s, w_c2, w_s2
+
+
+def products(c, s, c2, s2, x, y, x2, y2):
+    pairs = ((x * c, x2 * c2), (y * c, y2 * c2), (x * s, x2 * s2), (y * s, y2 * s2))
+    return [jnp.concatenate(pair, 0) for pair in pairs]
+
+
+def put_split(ref, at, i, parts):
+    lanes = slice(i * 128, i * 128 + 128)
+    for j, part in enumerate(parts):
+        top, bottom = split_bf16(part)
+        ref[at, j * 16 : j * 16 + 16, lanes] = top
+        ref[at, 64 + j * 16 : 80 + j * 16, lanes] = bottom
+
+
+def right_kernel(uvw, right, table, stage, steps):
+    step = pl.program_id(0)
+
+    @pl.when(step == 0)
+    def _():
+        turn_fields(uvw, 3, table)
+
+    for block in range(10):
+        rows = pl.ds(pl.multiple_of(step * 80 + block * 8, 8), 8)
+        stage_coord(table[1, rows, :], stage, steps, block, 0)
+        stage_w(table[2, rows, :], stage, block, 16)
+        for i in range(8):
+            parts = products(*staged_row(stage, steps, block, i))
+            put_split(right, block // 2, block % 2 * 8 + i, parts)
+
+
+def grid_kernel(uvw, values, right, mix, out, table, valued, stage, steps, left, sums):
+    step = pl.program_id(0)
+
+    @pl.when(step == 0)
+    def _():
+        turn_fields(uvw, 3, table)
+        turn_fields(values, 2, valued)
+
+    total = jnp.zeros((128, 128), F32)
+    for block in range(10):
+        rows = pl.ds(pl.multiple_of(step * 80 + block * 8, 8), 8)
+        stage_coord(table[0, rows, :], stage, steps, block, 0)
+        stage_w(table[2, rows, :], stage, block, 16)
+        for i in range(8):
+            c, s, c2, s2, x, y, x2, y2 = staged_row(stage, steps, block, i)
+            row = pl.ds(step * 80 + block * 8 + i, 1)
+            re, im = valued[0, row, :], valued[1, row, :]
+            weighted = (*turned(x, y, re, im), *turned(x2, y2, re, im))
+            put_split(left, block // 2, block % 2 * 8 + i, products(c, s, c2, s2, *weighted))
+        if block % 2:
+            total = total + dot_nt(left[block // 2], right[block // 2])
+    sums[step] = (total[:64, :64] + total[64:, 64:]) + (total[:64, 64:] + total[64:, :64])
+
+    @pl.when(step == 7)
+    def _():
+        twice = jnp.concatenate([mix[...], mix[...]], 1).astype(BF16)
+        turned_sums = []
+        for k in range(8):
+            turned_sums.append(dot_nt(jnp.concatenate(split_bf16(sums[k]), 1), twice))
+        for k in range(8):
+            both = jnp.concatenate(split_bf16(turned_sums[k]), 0)
+            grid = lax.dot_general(twice, both, NN, preferred_element_type=F32)
+            out[k, 0] = grid[:32, :32] - grid[32:, 32:]
+            out[k, 1] = grid[:32, 32:] + grid[32:, :32]
+
+
+def right_tables(uvw):
+    return pl.pallas_call(
+        right_kernel,
+        grid=(8,),
+        in_specs=[pl.BlockSpec((1920, 128), lambda k: (0, 0))],
+        out_specs=pl.BlockSpec((5, 128, 2048), lambda k: (k, 0, 0)),
+        out_shape=jax.ShapeDtypeStruct((40, 128, 2048), BF16),
+        scratch_shapes=[
+            VMEM((3, 640, 128), F32),
+            VMEM((10, 384, 128), F32),
+            VMEM((10, 16, 128), F32),
+        ],
+        compiler_params=pltpu.CompilerParams(vmem_limit_bytes=40 << 20),
+        cost_estimate=pl.CostEstimate(
+            flops=3000000000, bytes_accessed=22000000, transcendentals=0
+        ),
+        name="right_tables",
+    )(uvw)
+
+
+def grid_records(uvw, values, right):
+    whole = lambda shape: pl.BlockSpec(shape, lambda k: (0,) * len(shape))
     return pl.pallas_call(
         grid_kernel,
-        in_specs=[spec, spec, spec],
-        out_specs=spec,
+        grid=(8,),
+        in_specs=[
+            whole((1920, 128)),
+            whole((1280, 128)),
+            pl.BlockSpec((5, 128, 2048), lambda k: (k, 0, 0)),
+            whole((64, 64)),
+        ],
+        out_specs=whole((8, 2, 32, 32)),
         out_shape=jax.ShapeDtypeStruct((8, 2, 32, 32), F32),
         scratch_shapes=[
-            VMEM((5, 640, 128), F32),
-            VMEM((10, 512, 128), F32),
-            VMEM((10, 32, 128), F32),
-            VMEM((80 // CHUNK, 128, lanes), BF16),
-            VMEM((80 // CHUNK, 128, lanes), BF16),
+            VMEM((3, 640, 128), F32),
+            VMEM((2, 640, 128), F32),
+            VMEM((10, 384, 128), F32),
+            VMEM((10, 16, 128), F32),
+            VMEM((5, 128, 2048), BF16),
+            VMEM((8, 64, 64), F32),
         ],
         compiler_params=pltpu.CompilerParams(vmem_limit_bytes=40 << 20),
-        cost_estimate=pl.CostEstimate(flops=3000000000, bytes_accessed=5000000, transcendentals=0),
+        cost_estimate=pl.CostEstimate(
+            flops=3000000000, bytes_accessed=25000000, transcendentals=0
+        ),
         name="gridding",
-    )(uvw, values, jnp.asarray(mixing()))
+    )(uvw, values, right, jnp.asarray(mixing()))
 
 
 def to_owners(block):
@@ -614,8 +653,9 @@
     values = sort_to_windows(
         [stokes], ((0, 0), (0, 1)), target, starts, True, "sort_values"
     )
+    right = right_tables(uvw)
     values = to_owners(values)
-    grids = grid_records(uvw, values)
+    grids = grid_records(uvw, values, right)
     return visibilities[None], grids.reshape(8, 2, 1024)
 
 

time: 135 us -> 126 us (0.933)
  blocking collectives: 24.5 us -> 0 us
  starting transfers between devices: 25.2 us -> 35 us
  Pallas kernels: 72.1 us -> 75.8 us
  waiting for transfers between devices: 4.08 us -> 6.22 us
    all_to_all x1 -> x0, blocking collectives: 24.5 us -> none  [to_owners(): lax.all_to_all(block.reshape(128, 1, rows * 128), AXES, split_axis=0, con...]
    all_to_all x2 -> x3, starting transfers between devices: 20.6 us -> 30.4 us  [to_owners(): lax.all_to_all(block.reshape(128, 1, rows * 128), AXES, split_axis=0, con...]
    pallas_call x1 -> x2, Pallas kernels: 30 us -> 32.9 us  [the longest x1 20.2 us: grid_records(): pl.pallas_call(grid_kernel, grid=(8,), in_specs=[whole((1920, 128)), whol...]
    all_to_all x2 -> x3, waiting for transfers between devices: 0.43 us -> 2.58 us  [to_owners(): lax.all_to_all(block.reshape(128, 1, rows * 128), AXES, split_axis=0, con...]
  transfers between devices with their start and end apart: 3 -> 4, of which waited for: 2 -> 3; matrix products, arithmetic and copies ran while one was open for 0% -> 0% of each run, Pallas kernels for 27% -> 40%
where the time goes in v3:
time: 126 us; the launch traced here: 125 us
  Pallas kernels  75.8 us (60%)
  starting transfers between devices  35 us (28%)
  local copies, waits for them, and re-layouts  7.37 us (6%)
  waiting for transfers between devices  6.22 us (5%)
    all_to_all x3, starting transfers between devices, to_owners(): lax.all_to_all(block.reshape(128, 1, rows * 128), AXES, split_axis=0, con...  30.4 us
    pallas_call x2, Pallas kernels, sort_to_windows(): pl.pallas_call(functools.partial(window_kernel, picks, masked), in_specs=...  29.1 us
    pallas_call x1, Pallas kernels, grid_records(): pl.pallas_call(grid_kernel, grid=(8,), in_specs=[whole((1920, 128)), whol...  20.2 us
    pallas_call x1, Pallas kernels, right_tables(): pl.pallas_call(right_kernel, grid=(8,), in_specs=[pl.BlockSpec((1920, 128...  12.7 us
    pallas_call x1, Pallas kernels, correlate(): pl.pallas_call(correlate_kernel, in_specs=[spec], out_specs=[spec, spec],...  5.72 us
    pallas_call x1, Pallas kernels, channelize(): pl.pallas_call(channel_kernel, grid=(4,), in_specs=[pl.BlockSpec((2, 8, 3...  5.49 us
    unnamed x22, local copies, waits for them, and re-layouts  5.36 us
    ppermute x1, starting transfers between devices, per_device(): earlier = lax.ppermute(tail, 'img', [(i, i + 1) for i in range(count - 1)])  4.59 us
  transfers between devices with their start and end apart: 4, of which 3 were waited for; matrix products, arithmetic and copies ran while one was open for 0% of the time, Pallas kernels for 40%

profile of v3, /device:TPU:1, one launch (start us, length us, event | category | flops | bytes accessed | tf_op | source)
XLA Modules:
  0.0 125.1 jit_solution(13152060974671939414)
XLA Ops:
  0.6 1.2 slice.3
  1.9 4.6 %collective-permute-start = (f32[2,3,32,384]{3,2,1,0:T(8,128)S(1)}, f32[2,3,32,384]{3,2,1,0:T(8,128)S(1)}, u32[]{:S(2)}, u32[]{:S(2)}) collective-permute-start(f32[2,3,32,384]{3,2,1,0:T(8,128)S(1)} %bitcast.28), channel_id=1, source_target_pairs={{0,1},{1,2},{2,3},{3,4},{4,5},{5,6},{6,7},{8,9},{9,10},{10,11},{11... | collective-permute-start | bytes 884744 | tf_op jit(solution)/shard_map/ppermute | solution.py:641
  6.5 3.6 %collective-permute-done.halo = f32[2,3,32,384]{3,2,1,0:T(8,128)S(1)} collective-permute-done((f32[2,3,32,384]{3,2,1,0:T(8,128)S(1)}, f32[2,3,32,384]{3,2,1,0:T(8,128)S(1)}, u32[]{:S(2)}, u32[]{:S(2)}) %collective-permute-start) | collective-permute-done | bytes 294944 | tf_op jit(solution)/shard_map/ppermute | solution.py:641
  10.1 1.9 %copy-done = f32[2,32,32,384]{3,2,1,0:T(8,128)S(1)} copy-done((f32[2,32,32,384]{3,2,1,0:T(8,128)S(1)}, f32[2,32,32,384]{3,2,1,0:T(8,128)}, u32[]{:S(2)}) %copy-start) | copy-done | bytes 3145752
  12.0 1.0 copy-done.2
  13.0 1.0 copy-done.3
  14.0 0.7 copy-done.8
  14.7 5.5 %channelizer.1 = f32[2048,128]{1,0:T(8,128)} custom-call(f32[2,32,32,384]{3,2,1,0:T(8,128)S(1)} %copy-done, f32[2,3,32,384]{3,2,1,0:T(8,128)S(1)} %collective-permute-done.halo, f32[4,384]{1,0:T(4,128)S(1)} %copy-done.8, bf16[256,768]{1,0:T(8,128)(2,1)S(1)} %copy-done.3, bf16[256,768]{1,0:T(8,128)(2,1)S(1)} %copy-done.2), custom_call_target="tpu_custom_call" | custom-call | flops 1200000000 | bytes 6000000 | tf_op jit(solution)/shard_map/channelizer/pallas_call | solution.py:83
  20.2 11.3 %all-to-all-start = ((f32[128,1,2048]{2,1,0:T(1,128)}), f32[128,1,2048]{2,1,0:T(1,128)S(1)}, u32[]{:S(2)}, u32[]{:S(2)}) async-start(f32[128,1,2048]{2,1,0:T(1,128)} %bitcast.1), calls=%async_computation | async-start | bytes 2097152 | tf_op jit(solution)/shard_map/all_to_all | solution.py:632
  31.5 2.6 %record_starts.1.args_3_.args_2_ = s32[32,32]{1,0:T(8,128)} custom-call(s32[320,128]{1,0:T(8,128)} %bitcast.23), custom_call_target="tpu_custom_call" | custom-call | flops 100000000 | bytes 200000 | tf_op jit(solution)/shard_map/record_starts/pallas_call | solution.py:239
  34.1 0.7 copy-done.5
  34.9 15.3 %sort_places.1 = f32[1920,128]{1,0:T(8,128)} custom-call(f32[2,320,128]{2,1,0:T(8,128)S(1)} %bitcast.21, f32[1,320,128]{2,1,0:T(8,128)S(1)} %bitcast.26, s32[320,128]{1,0:T(8,128)S(1)} %bitcast.24, s32[32,32]{1,0:T(8,128)S(1)} %copy-done.5), custom_call_target="tpu_custom_call" | custom-call | flops 200000000 | bytes 9000000 | tf_op jit(solution)/shard_map/sort_places/pallas_call | solution.py:404
  50.1 0.4 all-to-all-done
  50.6 9.3 %all-to-all-start.1 = ((f32[128,1,1920]{2,1,0:T(1,128)}), f32[128,1,1920]{2,1,0:T(1,128)S(1)}, u32[]{:S(2)}, u32[]{:S(2)}) async-start(f32[128,1,1920]{2,1,0:T(1,128)} %bitcast.6), calls=%async_computation.1 | async-start | bytes 1966080 | tf_op jit(solution)/shard_map/all_to_all | solution.py:632
  59.9 0.0 copy-start.6
  59.9 5.7 %correlator.1 = (f32[10,2,128,128]{3,2,1,0:T(8,128)}, f32[2,320,128]{2,1,0:T(8,128)S(1)}) custom-call(f32[2048,128]{1,0:T(8,128)S(1)} %bitcast.22), custom_call_target="tpu_custom_call" | custom-call | flops 4000000000 | bytes 4000000 | tf_op jit(solution)/shard_map/correlator/pallas_call | solution.py:188
  65.7 13.8 %sort_values.1 = f32[1280,128]{1,0:T(8,128)} custom-call(f32[2,320,128]{2,1,0:T(8,128)S(1)} %get-tuple-element.5.args_0_, s32[320,128]{1,0:T(8,128)S(1)} %bitcast.25, s32[32,32]{1,0:T(8,128)S(1)} %copy-done.6), custom_call_target="tpu_custom_call" | custom-call | flops 200000000 | bytes 6000000 | tf_op jit(solution)/shard_map/sort_values/pallas_call | solution.py:404
  79.5 0.0 all-to-all-done.1
  79.5 9.8 %all-to-all-start.2 = ((f32[128,1,1280]{2,1,0:T(1,128)}), f32[128,1,1280]{2,1,0:T(1,128)S(1)}, u32[]{:S(2)}, u32[]{:S(2)}) async-start(f32[128,1,1280]{2,1,0:T(1,128)} %bitcast.8), calls=%async_computation.2 | async-start | bytes 1310720 | tf_op jit(solution)/shard_map/all_to_all | solution.py:632
  89.3 0.0 copy-start.7
  89.3 12.7 %right_tables.1.right = bf16[40,128,2048]{2,1,0:T(8,128)(2,1)} custom-call(f32[1920,128]{1,0:T(8,128)S(1)} %bitcast.18), custom_call_target="tpu_custom_call" | custom-call | flops 3000000000 | bytes 22000000 | tf_op jit(solution)/shard_map/right_tables/pallas_call | solution.py:582
  102.0 2.2 %all-to-all-done.2 = f32[128,1,1280]{2,1,0:T(1,128)S(1)} async-done(((f32[128,1,1280]{2,1,0:T(1,128)}), f32[128,1,1280]{2,1,0:T(1,128)S(1)}, u32[]{:S(2)}, u32[]{:S(2)}) %all-to-all-start.2) | async-done | bytes 655392 | tf_op jit(solution)/shard_map/all_to_all | solution.py:632
  104.1 20.2 %gridding.1 = f32[8,2,32,32]{3,2,1,0:T(8,128)S(1)} custom-call(f32[1920,128]{1,0:T(8,128)S(1)} %bitcast.19, f32[1280,128]{1,0:T(8,128)S(1)} %bitcast.20, bf16[40,128,2048]{2,1,0:T(8,128)(2,1)} %right_tables.1.right, f32[64,64]{1,0:T(8,128)S(1)} %copy-done.7), custom_call_target="tpu_custom_call" | custom-call | flops 3000000000 | bytes 25000000 | tf_op jit(solution)/shard_map/gridding/pallas_call | solution.py:603
  124.3 0.8 reshape.43
  (15 shorter events, 0.1 us)
Async XLA Ops:
  1.9 8.2 %collective-permute-start = (f32[2,3,32,384]{3,2,1,0:T(8,128)S(1)}, f32[2,3,32,384]{3,2,1,0:T(8,128)S(1)}, u32[]{:S(2)}, u32[]{:S(2)}) collective-permute-start(f32[2,3,32,384]{3,2,1,0:T(8,128)S(1)} %bitcast.28), channel_id=1, source_target_pairs={{0,1},{1,2},{2,3},{3,4},{4,5},{5,6},{6,7},{8,9},{9,10},{10,11},{11... | collective-permute-start | bytes 884744 | tf_op jit(solution)/shard_map/ppermute | solution.py:641
  10.1 1.9 %copy-start = (f32[2,32,32,384]{3,2,1,0:T(8,128)S(1)}, f32[2,32,32,384]{3,2,1,0:T(8,128)}, u32[]{:S(2)}) copy-start(f32[2,32,32,384]{3,2,1,0:T(8,128)} %volt.1) | copy-start | bytes 9437188
  12.0 1.0 copy-start.2
  13.0 1.0 copy-start.3
  14.0 0.7 copy-start.8
  14.7 16.8 %copy-start.9 = (f32[2,40960]{1,0:T(2,128)S(1)}, f32[2,40960]{1,0:T(2,128)}, u32[]{:S(2)}) copy-start(f32[2,40960]{1,0:T(2,128)} %param.10) | copy-start | bytes 983044
  14.7 19.4 %copy-start.1 = (s32[40960,1]{0,1:T(1,128)S(1)}, s32[40960,1]{0,1:T(1,128)}, u32[]{:S(2)}) copy-start(s32[40960,1]{0,1:T(1,128)} %param.12) | copy-start | bytes 491524
  14.7 19.4 %copy-start.4 = (f32[40960]{0:T(1024)S(1)}, f32[40960]{0:T(1024)}, u32[]{:S(2)}) copy-start(f32[40960]{0:T(1024)} %param.11) | copy-start | bytes 491524
  20.2 30.4 %all-to-all-start = ((f32[128,1,2048]{2,1,0:T(1,128)}), f32[128,1,2048]{2,1,0:T(1,128)S(1)}, u32[]{:S(2)}, u32[]{:S(2)}) async-start(f32[128,1,2048]{2,1,0:T(1,128)} %bitcast.1), calls=%async_computation | async-start | bytes 2097152 | tf_op jit(solution)/shard_map/all_to_all | solution.py:632
  34.1 0.7 copy-start.5
  50.6 28.9 %all-to-all-start.1 = ((f32[128,1,1920]{2,1,0:T(1,128)}), f32[128,1,1920]{2,1,0:T(1,128)S(1)}, u32[]{:S(2)}, u32[]{:S(2)}) async-start(f32[128,1,1920]{2,1,0:T(1,128)} %bitcast.6), calls=%async_computation.1 | async-start | bytes 1966080 | tf_op jit(solution)/shard_map/all_to_all | solution.py:632
  59.9 5.7 %copy-start.6 = (s32[32,32]{1,0:T(8,128)S(1)}, s32[32,32]{1,0:T(8,128)}, u32[]{:S(2)}) copy-start(s32[32,32]{1,0:T(8,128)} %record_starts.1.args_3_.args_2_) | copy-start | bytes 12292
  79.5 24.7 %all-to-all-start.2 = ((f32[128,1,1280]{2,1,0:T(1,128)}), f32[128,1,1280]{2,1,0:T(1,128)S(1)}, u32[]{:S(2)}, u32[]{:S(2)}) async-start(f32[128,1,1280]{2,1,0:T(1,128)} %bitcast.8), calls=%async_computation.2 | async-start | bytes 1310720 | tf_op jit(solution)/shard_map/all_to_all | solution.py:632
  89.3 14.9 %copy-start.7 = (f32[64,64]{1,0:T(8,128)S(1)}, f32[64,64]{1,0:T(8,128)}, u32[]{:S(2)}) copy-start(f32[64,64]{1,0:T(8,128)} %constant.8.clone.mix) | copy-start | bytes 49156

commit v4 on v3

--- a/solution.py
+++ b/solution.py
@@ -97,7 +97,7 @@
             VMEM((2, 128, 768), BF16),
             VMEM((2, 128, 768), BF16),
         ],
-        compiler_params=pltpu.CompilerParams(vmem_limit_bytes=40 << 20),
+        compiler_params=pltpu.CompilerParams(vmem_limit_bytes=60 << 20),
         cost_estimate=pl.CostEstimate(flops=1200000000, bytes_accessed=6000000, transcendentals=0),
         name="channelizer",
     )(voltages, halo, prototype, jnp.asarray(high), jnp.asarray(low))
@@ -230,8 +230,10 @@
     start = jnp.minimum(start, 40959.0)
     line = jnp.floor((start + 0.5) * (1.0 / 320.0))
     place = start - line * 320.0
-    code = total * 65536.0 + line * 512.0 + place
-    out[...] = code.astype(I32)
+    tile = jnp.floor(place * (1.0 / 128.0))
+    row = (tile * 1024.0 + line * 8.0).astype(I32)
+    shift = (place - tile * 128.0).astype(I32)
+    out[...] = (total.astype(I32) << 20) | (shift << 13) | row
 
 
 def record_starts(target):
@@ -372,18 +374,19 @@
             jnp.concatenate([after[64:], after[64:]], 0),
         ]
         for t in range(4):
-            zext[t, pl.ds(f, 128, stride=8), :] = tiles[t].T
+            zext[pl.ds(t * 1024 + f, 128, stride=8), :] = tiles[t].T
 
     def windows(step, carry):
-        for near in range(4):
-            d = step * 4 + near
+        for near in range(8):
+            d = step * 8 + near
             tiles = [None] * 5
             for k in range(8):
-                code = starts[step, near * 8 + k]
-                count, line, place = code >> 16, (code >> 9) & 127, code & 511
-                tile, shift = place >> 7, place & 127
-                rows = pl.ds(pl.multiple_of(line * 8, 8), 8)
-                joined = jnp.where(lan >= shift, zext[tile, rows, :], zext[tile + 1, rows, :])
+                code = starts[step * 2 + near // 4, near % 4 * 8 + k]
+                count, shift = code >> 20, (code >> 13) & 127
+                row = pl.multiple_of(code & 8191, 8)
+                joined = jnp.where(
+                    lan >= shift, zext[pl.ds(row, 8), :], zext[pl.ds(row + 1024, 8), :]
+                )
                 index, offset = (80 * k) // 128, (80 * k) % 128
                 value = pltpu.roll(joined, (offset - shift) & 127, 1)
                 if masked:
@@ -395,7 +398,7 @@
                 out[pl.ds(d * (5 * n) + t * n, n), :] = tiles[t][:n]
         return carry
 
-    lax.fori_loop(0, 32, windows, 0)
+    lax.fori_loop(0, 16, windows, 0)
 
 
 def sort_to_windows(files, picks, target, starts, masked, name):
@@ -411,7 +414,7 @@
             VMEM((n, 320, 128), F32),
             VMEM((384, 128), I32),
             VMEM((n, 384, 128), F32),
-            VMEM((4, 1024, 128), F32),
+            VMEM((4096, 128), F32),
         ],
         compiler_params=pltpu.CompilerParams(vmem_limit_bytes=32 << 20),
         cost_estimate=pl.CostEstimate(flops=200000000, bytes_accessed=3000000 * n, transcendentals=0),
@@ -542,7 +545,7 @@
             put_split(right, block // 2, block % 2 * 8 + i, parts)
 
 
-def grid_kernel(uvw, values, right, mix, out, table, valued, stage, steps, left, sums):
+def grid_kernel(uvw, values, right, mix, out, table, valued, stage, steps, sums):
     step = pl.program_id(0)
 
     @pl.when(step == 0)
@@ -551,6 +554,7 @@
         turn_fields(values, 2, valued)
 
     total = jnp.zeros((128, 128), F32)
+    held = []
     for block in range(10):
         rows = pl.ds(pl.multiple_of(step * 80 + block * 8, 8), 8)
         stage_coord(table[0, rows, :], stage, steps, block, 0)
@@ -560,9 +564,12 @@
             row = pl.ds(step * 80 + block * 8 + i, 1)
             re, im = valued[0, row, :], valued[1, row, :]
             weighted = (*turned(x, y, re, im), *turned(x2, y2, re, im))
-            put_split(left, block // 2, block % 2 * 8 + i, products(c, s, c2, s2, *weighted))
-        if block % 2:
-            total = total + dot_nt(left[block // 2], right[block // 2])
+            halves = [split_bf16(x) for x in products(c, s, c2, s2, *weighted)]
+            held.append(jnp.concatenate([x for x, _ in halves] + [y for _, y in halves], 0))
+            if i % 2:
+                at = (block % 2 * 8 + i + 1) * 128
+                pair = right[block // 2, :, at - 256 : at]
+                total = total + dot_nt(jnp.concatenate(held[-2:], 1), pair)
     sums[step] = (total[:64, :64] + total[64:, 64:]) + (total[:64, 64:] + total[64:, :64])
 
     @pl.when(step == 7)
@@ -616,7 +623,6 @@
             VMEM((2, 640, 128), F32),
             VMEM((10, 384, 128), F32),
             VMEM((10, 16, 128), F32),
-            VMEM((5, 128, 2048), BF16),
             VMEM((8, 64, 64), F32),
         ],
         compiler_params=pltpu.CompilerParams(vmem_limit_bytes=40 << 20),

time: 126 us -> 116 us (0.921)
  Pallas kernels: 75.8 us -> 69.7 us
  local copies, waits for them, and re-layouts: 7.37 us -> 3.51 us
  waiting for transfers between devices: 6.22 us -> 9.46 us
  starting transfers between devices: 35 us -> 31.9 us
    pallas_call x2, Pallas kernels: 29.1 us -> 24.7 us  [sort_to_windows(): pl.pallas_call(functools.partial(window_kernel, picks, masked), in_specs=...]
    unnamed x22 -> x16, local copies, waits for them, and re-layouts: 5.36 us -> 1.5 us
    all_to_all x3, waiting for transfers between devices: 2.58 us -> 5.81 us  [to_owners(): lax.all_to_all(block.reshape(128, 1, rows * 128), AXES, split_axis=0, con...]
    all_to_all x3, starting transfers between devices: 30.4 us -> 27.2 us  [to_owners(): lax.all_to_all(block.reshape(128, 1, rows * 128), AXES, split_axis=0, con...]
    pallas_call x1, Pallas kernels: 20.2 us -> 17.2 us  [grid_records(): pl.pallas_call(grid_kernel, grid=(8,), in_specs=[whole((1920, 128)), whol...]
  transfers between devices with their start and end apart: 4 -> 4, of which waited for: 3 -> 4; matrix products, arithmetic and copies ran while one was open for 0% -> 0% of each run, Pallas kernels for 40% -> 40%
where the time goes in v4:
time: 116 us; the launch traced here: 115 us
  Pallas kernels  69.7 us (60%)
  starting transfers between devices  31.9 us (28%)
  waiting for transfers between devices  9.46 us (8%)
  local copies, waits for them, and re-layouts  3.51 us (3%)
    all_to_all x3, starting transfers between devices, to_owners(): lax.all_to_all(block.reshape(128, 1, rows * 128), AXES, split_axis=0, con...  27.2 us
    pallas_call x2, Pallas kernels, sort_to_windows(): pl.pallas_call(functools.partial(window_kernel, picks, masked), in_specs=...  24.7 us
    pallas_call x1, Pallas kernels, grid_records(): pl.pallas_call(grid_kernel, grid=(8,), in_specs=[whole((1920, 128)), whol...  17.2 us
    pallas_call x1, Pallas kernels, right_tables(): pl.pallas_call(right_kernel, grid=(8,), in_specs=[pl.BlockSpec((1920, 128...  12.7 us
    pallas_call x1, Pallas kernels, channelize(): pl.pallas_call(channel_kernel, grid=(4,), in_specs=[pl.BlockSpec((2, 8, 3...  6.7 us
    all_to_all x3, waiting for transfers between devices, to_owners(): lax.all_to_all(block.reshape(128, 1, rows * 128), AXES, split_axis=0, con...  5.81 us
    pallas_call x1, Pallas kernels, correlate(): pl.pallas_call(correlate_kernel, in_specs=[spec], out_specs=[spec, spec],...  5.72 us
    ppermute x1, starting transfers between devices, per_device(): earlier = lax.ppermute(tail, 'img', [(i, i + 1) for i in range(count - 1)])  4.73 us
  transfers between devices with their start and end apart: 4, of which 4 were waited for; matrix products, arithmetic and copies ran while one was open for 0% of the time, Pallas kernels for 40%

profile of v4, /device:TPU:1, one launch (start us, length us, event | category | flops | bytes accessed | tf_op | source)
XLA Modules:
  0.0 115.3 jit_solution(11469600053385316207)
XLA Ops:
  0.6 1.2 %slice.3 = f32[2,32,3,384]{3,2,1,0:T(4,128)S(1)} slice(f32[2,32,32,384]{3,2,1,0:T(8,128)} %volt.1), slice={[0:2], [0:32], [29:32], [0:384]} | slice | bytes 589824 | tf_op jit(solution)/shard_map/slice | solution.py:645
  1.9 0.0 copy-start.5
  1.9 0.0 copy-start
  1.9 0.0 copy-start.1
  1.9 4.7 %collective-permute-start = (f32[2,3,32,384]{3,2,1,0:T(8,128)S(1)}, f32[2,3,32,384]{3,2,1,0:T(8,128)S(1)}, u32[]{:S(2)}, u32[]{:S(2)}) collective-permute-start(f32[2,3,32,384]{3,2,1,0:T(8,128)S(1)} %bitcast.29), channel_id=1, source_target_pairs={{0,1},{1,2},{2,3},{3,4},{4,5},{5,6},{6,7},{8,9},{9,10},{10,11},{11... | collective-permute-start | bytes 884744 | tf_op jit(solution)/shard_map/ppermute | solution.py:647
  6.7 3.6 %collective-permute-done.halo = f32[2,3,32,384]{3,2,1,0:T(8,128)S(1)} collective-permute-done((f32[2,3,32,384]{3,2,1,0:T(8,128)S(1)}, f32[2,3,32,384]{3,2,1,0:T(8,128)S(1)}, u32[]{:S(2)}, u32[]{:S(2)}) %collective-permute-start) | collective-permute-done | bytes 294944 | tf_op jit(solution)/shard_map/ppermute | solution.py:647
  10.3 0.7 copy-done.6
  11.0 6.7 %channelizer.1 = f32[2048,128]{1,0:T(8,128)} custom-call(f32[2,32,32,384]{3,2,1,0:T(8,128)} %volt.1, f32[2,3,32,384]{3,2,1,0:T(8,128)} %copy-done.6, f32[4,384]{1,0:T(4,128)} %proto.1, bf16[256,768]{1,0:T(8,128)(2,1)} %constant.6.clone.table_high, bf16[256,768]{1,0:T(8,128)(2,1)} %constant.7.clone.table_low), custom_call_target="tpu_custom_call" | custom-call | flops 1200000000 | bytes 6000000 | tf_op jit(solution)/shard_map/channelizer/pallas_call | solution.py:83
  17.7 11.3 %all-to-all-start = ((f32[128,1,2048]{2,1,0:T(1,128)}), f32[128,1,2048]{2,1,0:T(1,128)S(1)}, u32[]{:S(2)}, u32[]{:S(2)}) async-start(f32[128,1,2048]{2,1,0:T(1,128)} %bitcast.27), calls=%async_computation | async-start | bytes 2097152 | tf_op jit(solution)/shard_map/all_to_all | solution.py:638
  29.0 2.6 %record_starts.1.args_3_.args_2_ = s32[32,32]{1,0:T(8,128)} custom-call(s32[320,128]{1,0:T(8,128)} %bitcast.23), custom_call_target="tpu_custom_call" | custom-call | flops 100000000 | bytes 200000 | tf_op jit(solution)/shard_map/record_starts/pallas_call | solution.py:241
  31.7 0.7 copy-done.2
  32.4 13.0 %sort_places.1 = f32[1920,128]{1,0:T(8,128)} custom-call(f32[2,320,128]{2,1,0:T(8,128)S(1)} %bitcast.21, f32[1,320,128]{2,1,0:T(8,128)S(1)} %bitcast.26, s32[320,128]{1,0:T(8,128)S(1)} %bitcast.24, s32[32,32]{1,0:T(8,128)S(1)} %copy-done.2), custom_call_target="tpu_custom_call" | custom-call | flops 200000000 | bytes 9000000 | tf_op jit(solution)/shard_map/sort_places/pallas_call | solution.py:407
  45.4 2.7 %all-to-all-done = f32[128,1,2048]{2,1,0:T(1,128)S(1)} async-done(((f32[128,1,2048]{2,1,0:T(1,128)}), f32[128,1,2048]{2,1,0:T(1,128)S(1)}, u32[]{:S(2)}, u32[]{:S(2)}) %all-to-all-start) | async-done | bytes 1048608 | tf_op jit(solution)/shard_map/all_to_all | solution.py:638
  48.1 7.1 %all-to-all-start.1 = ((f32[128,1,1920]{2,1,0:T(1,128)}), f32[128,1,1920]{2,1,0:T(1,128)S(1)}, u32[]{:S(2)}, u32[]{:S(2)}) async-start(f32[128,1,1920]{2,1,0:T(1,128)} %bitcast.6), calls=%async_computation.1 | async-start | bytes 1966080 | tf_op jit(solution)/shard_map/all_to_all | solution.py:638
  55.2 0.0 copy-start.3
  55.2 5.7 %correlator.1 = (f32[10,2,128,128]{3,2,1,0:T(8,128)}, f32[2,320,128]{2,1,0:T(8,128)S(1)}) custom-call(f32[2048,128]{1,0:T(8,128)S(1)} %bitcast.22), custom_call_target="tpu_custom_call" | custom-call | flops 4000000000 | bytes 4000000 | tf_op jit(solution)/shard_map/correlator/pallas_call | solution.py:188
  60.9 11.6 %sort_values.1 = f32[1280,128]{1,0:T(8,128)} custom-call(f32[2,320,128]{2,1,0:T(8,128)S(1)} %get-tuple-element.5.args_0_, s32[320,128]{1,0:T(8,128)S(1)} %bitcast.25, s32[32,32]{1,0:T(8,128)S(1)} %copy-done.3), custom_call_target="tpu_custom_call" | custom-call | flops 200000000 | bytes 6000000 | tf_op jit(solution)/shard_map/sort_values/pallas_call | solution.py:407
  72.6 1.0 all-to-all-done.1
  73.6 8.8 %all-to-all-start.2 = ((f32[128,1,1280]{2,1,0:T(1,128)}), f32[128,1,1280]{2,1,0:T(1,128)S(1)}, u32[]{:S(2)}, u32[]{:S(2)}) async-start(f32[128,1,1280]{2,1,0:T(1,128)} %bitcast.8), calls=%async_computation.2 | async-start | bytes 1310720 | tf_op jit(solution)/shard_map/all_to_all | solution.py:638
  82.4 0.0 copy-start.4
  82.4 12.7 %right_tables.1.right = bf16[40,128,2048]{2,1,0:T(8,128)(2,1)} custom-call(f32[1920,128]{1,0:T(8,128)S(1)} %bitcast.18), custom_call_target="tpu_custom_call" | custom-call | flops 3000000000 | bytes 22000000 | tf_op jit(solution)/shard_map/right_tables/pallas_call | solution.py:589
  95.1 2.2 %all-to-all-done.2 = f32[128,1,1280]{2,1,0:T(1,128)S(1)} async-done(((f32[128,1,1280]{2,1,0:T(1,128)}), f32[128,1,1280]{2,1,0:T(1,128)S(1)}, u32[]{:S(2)}, u32[]{:S(2)}) %all-to-all-start.2) | async-done | bytes 655392 | tf_op jit(solution)/shard_map/all_to_all | solution.py:638
  97.3 17.2 %gridding.1 = f32[8,2,32,32]{3,2,1,0:T(8,128)S(1)} custom-call(f32[1920,128]{1,0:T(8,128)S(1)} %bitcast.19, f32[1280,128]{1,0:T(8,128)S(1)} %bitcast.20, bf16[40,128,2048]{2,1,0:T(8,128)(2,1)} %right_tables.1.right, f32[64,64]{1,0:T(8,128)S(1)} %copy-done.4), custom_call_target="tpu_custom_call" | custom-call | flops 3000000000 | bytes 25000000 | tf_op jit(solution)/shard_map/gridding/pallas_call | solution.py:610
  114.5 0.8 reshape.43
  (9 shorter events, 0.1 us)
Async XLA Ops:
  1.9 27.1 %copy-start.5 = (f32[2,40960]{1,0:T(2,128)S(1)}, f32[2,40960]{1,0:T(2,128)}, u32[]{:S(2)}) copy-start(f32[2,40960]{1,0:T(2,128)} %param.10) | copy-start | bytes 983044
  1.9 29.8 %copy-start = (s32[40960,1]{0,1:T(1,128)S(1)}, s32[40960,1]{0,1:T(1,128)}, u32[]{:S(2)}) copy-start(s32[40960,1]{0,1:T(1,128)} %param.12) | copy-start | bytes 491524
  1.9 29.7 %copy-start.1 = (f32[40960]{0:T(1024)S(1)}, f32[40960]{0:T(1024)}, u32[]{:S(2)}) copy-start(f32[40960]{0:T(1024)} %param.11) | copy-start | bytes 491524
  1.9 8.4 %collective-permute-start = (f32[2,3,32,384]{3,2,1,0:T(8,128)S(1)}, f32[2,3,32,384]{3,2,1,0:T(8,128)S(1)}, u32[]{:S(2)}, u32[]{:S(2)}) collective-permute-start(f32[2,3,32,384]{3,2,1,0:T(8,128)S(1)} %bitcast.29), channel_id=1, source_target_pairs={{0,1},{1,2},{2,3},{3,4},{4,5},{5,6},{6,7},{8,9},{9,10},{10,11},{11... | collective-permute-start | bytes 884744 | tf_op jit(solution)/shard_map/ppermute | solution.py:647
  10.3 0.7 copy-start.6
  17.7 30.4 %all-to-all-start = ((f32[128,1,2048]{2,1,0:T(1,128)}), f32[128,1,2048]{2,1,0:T(1,128)S(1)}, u32[]{:S(2)}, u32[]{:S(2)}) async-start(f32[128,1,2048]{2,1,0:T(1,128)} %bitcast.27), calls=%async_computation | async-start | bytes 2097152 | tf_op jit(solution)/shard_map/all_to_all | solution.py:638
  31.7 0.7 copy-start.2
  48.1 25.5 %all-to-all-start.1 = ((f32[128,1,1920]{2,1,0:T(1,128)}), f32[128,1,1920]{2,1,0:T(1,128)S(1)}, u32[]{:S(2)}, u32[]{:S(2)}) async-start(f32[128,1,1920]{2,1,0:T(1,128)} %bitcast.6), calls=%async_computation.1 | async-start | bytes 1966080 | tf_op jit(solution)/shard_map/all_to_all | solution.py:638
  55.2 5.7 %copy-start.3 = (s32[32,32]{1,0:T(8,128)S(1)}, s32[32,32]{1,0:T(8,128)}, u32[]{:S(2)}) copy-start(s32[32,32]{1,0:T(8,128)} %record_starts.1.args_3_.args_2_) | copy-start | bytes 12292
  73.6 23.7 %all-to-all-start.2 = ((f32[128,1,1280]{2,1,0:T(1,128)}), f32[128,1,1280]{2,1,0:T(1,128)S(1)}, u32[]{:S(2)}, u32[]{:S(2)}) async-start(f32[128,1,1280]{2,1,0:T(1,128)} %bitcast.8), calls=%async_computation.2 | async-start | bytes 1310720 | tf_op jit(solution)/shard_map/all_to_all | solution.py:638
  82.4 14.9 %copy-start.4 = (f32[64,64]{1,0:T(8,128)S(1)}, f32[64,64]{1,0:T(8,128)}, u32[]{:S(2)}) copy-start(f32[64,64]{1,0:T(8,128)} %constant.8.clone.mix) | copy-start | bytes 49156

commit v5 on v4

--- a/solution.py
+++ b/solution.py
@@ -106,7 +106,7 @@
 def correlate_kernel(recv, vis, stokes, a_ref, hh, hl, xlh, xll, xrh, xrl):
     lane = lax.broadcasted_iota(I32, (8, 128), 1) >> 5
 
-    def turn(stn, carry):
+    def turn(stn):
         for h in range(2):
             for q in range(2):
                 parts = []
@@ -120,9 +120,13 @@
                         moved = pltpu.roll(parts[m], shift, 1) if shift else parts[m]
                         joined = moved if joined is None else jnp.where(lane == m, moved, joined)
                     a_ref[q, h, pl.ds(stn * 32 + b, 8, stride=4), :] = joined
+
+    def turn_four(step, carry):
+        for near in range(4):
+            turn(step * 4 + near)
         return carry
 
-    lax.fori_loop(0, 16, turn, 0)
+    lax.fori_loop(0, 4, turn_four, 0)
 
     for q in range(2):
         for h in range(2):
@@ -545,12 +549,11 @@
             put_split(right, block // 2, block % 2 * 8 + i, parts)
 
 
-def grid_kernel(uvw, values, right, mix, out, table, valued, stage, steps, sums):
+def grid_kernel(values, right, table, mix, out, valued, stage, steps, sums):
     step = pl.program_id(0)
 
     @pl.when(step == 0)
     def _():
-        turn_fields(uvw, 3, table)
         turn_fields(values, 2, valued)
 
     total = jnp.zeros((128, 128), F32)
@@ -590,14 +593,19 @@
         right_kernel,
         grid=(8,),
         in_specs=[pl.BlockSpec((1920, 128), lambda k: (0, 0))],
-        out_specs=pl.BlockSpec((5, 128, 2048), lambda k: (k, 0, 0)),
-        out_shape=jax.ShapeDtypeStruct((40, 128, 2048), BF16),
+        out_specs=[
+            pl.BlockSpec((5, 128, 2048), lambda k: (k, 0, 0)),
+            pl.BlockSpec((3, 640, 128), lambda k: (0, 0, 0)),
+        ],
+        out_shape=[
+            jax.ShapeDtypeStruct((40, 128, 2048), BF16),
+            jax.ShapeDtypeStruct((3, 640, 128), F32),
+        ],
         scratch_shapes=[
-            VMEM((3, 640, 128), F32),
             VMEM((10, 384, 128), F32),
             VMEM((10, 16, 128), F32),
         ],
-        compiler_params=pltpu.CompilerParams(vmem_limit_bytes=40 << 20),
+        compiler_params=pltpu.CompilerParams(vmem_limit_bytes=24 << 20),
         cost_estimate=pl.CostEstimate(
             flops=3000000000, bytes_accessed=22000000, transcendentals=0
         ),
@@ -605,32 +613,31 @@
     )(uvw)
 
 
-def grid_records(uvw, values, right):
+def grid_records(values, right, table):
     whole = lambda shape: pl.BlockSpec(shape, lambda k: (0,) * len(shape))
     return pl.pallas_call(
         grid_kernel,
         grid=(8,),
         in_specs=[
-            whole((1920, 128)),
             whole((1280, 128)),
             pl.BlockSpec((5, 128, 2048), lambda k: (k, 0, 0)),
+            whole((3, 640, 128)),
             whole((64, 64)),
         ],
         out_specs=whole((8, 2, 32, 32)),
         out_shape=jax.ShapeDtypeStruct((8, 2, 32, 32), F32),
         scratch_shapes=[
-            VMEM((3, 640, 128), F32),
             VMEM((2, 640, 128), F32),
             VMEM((10, 384, 128), F32),
             VMEM((10, 16, 128), F32),
             VMEM((8, 64, 64), F32),
         ],
-        compiler_params=pltpu.CompilerParams(vmem_limit_bytes=40 << 20),
+        compiler_params=pltpu.CompilerParams(vmem_limit_bytes=24 << 20),
         cost_estimate=pl.CostEstimate(
             flops=3000000000, bytes_accessed=25000000, transcendentals=0
         ),
         name="gridding",
-    )(uvw, values, right, jnp.asarray(mixing()))
+    )(values, right, table, jnp.asarray(mixing()))
 
 
 def to_owners(block):
@@ -659,9 +666,9 @@
     values = sort_to_windows(
         [stokes], ((0, 0), (0, 1)), target, starts, True, "sort_values"
     )
-    right = right_tables(uvw)
+    tables = right_tables(uvw)
     values = to_owners(values)
-    grids = grid_records(uvw, values, right)
+    grids = grid_records(values, *tables)
     return visibilities[None], grids.reshape(8, 2, 1024)
 
 

time: 116 us -> 123 us (1.060)
  local copies, waits for them, and re-layouts: 3.51 us -> 17.4 us
  Pallas kernels: 69.7 us -> 64.6 us
  waiting for transfers between devices: 9.46 us -> 8.11 us
    unnamed x16 -> x20, local copies, waits for them, and re-layouts: 1.5 us -> 15.4 us
    pallas_call x1, Pallas kernels: 12.7 us -> 10.5 us  [right_tables(): pl.pallas_call(right_kernel, grid=(8,), in_specs=[pl.BlockSpec((1920, 128...]
    pallas_call x1, Pallas kernels: 17.2 us -> 15.2 us  [grid_records(): pl.pallas_call(grid_kernel, grid=(8,), in_specs=[whole((1280, 128)), pl.B...]
    all_to_all x3, waiting for transfers between devices: 5.81 us -> 4.47 us  [to_owners(): lax.all_to_all(block.reshape(128, 1, rows * 128), AXES, split_axis=0, con...]
  transfers between devices with their start and end apart: 4 -> 4, of which waited for: 4 -> 3; matrix products, arithmetic and copies ran while one was open for 0% -> 0% of each run, Pallas kernels for 40% -> 35%
where the time goes in v5:
time: 123 us; the launch traced here: 122 us
  Pallas kernels  64.6 us (53%)
  starting transfers between devices  31.1 us (25%)
  local copies, waits for them, and re-layouts  17.4 us (14%)
  waiting for transfers between devices  8.11 us (7%)
    all_to_all x3, starting transfers between devices, to_owners(): lax.all_to_all(block.reshape(128, 1, rows * 128), AXES, split_axis=0, con...  26.4 us
    pallas_call x2, Pallas kernels, sort_to_windows(): pl.pallas_call(functools.partial(window_kernel, picks, masked), in_specs=...  24.7 us
    unnamed x20, local copies, waits for them, and re-layouts  15.4 us
    pallas_call x1, Pallas kernels, grid_records(): pl.pallas_call(grid_kernel, grid=(8,), in_specs=[whole((1280, 128)), pl.B...  15.2 us
    pallas_call x1, Pallas kernels, right_tables(): pl.pallas_call(right_kernel, grid=(8,), in_specs=[pl.BlockSpec((1920, 128...  10.5 us
    pallas_call x1, Pallas kernels, channelize(): pl.pallas_call(channel_kernel, grid=(4,), in_specs=[pl.BlockSpec((2, 8, 3...  6.7 us
    pallas_call x1, Pallas kernels, correlate(): pl.pallas_call(correlate_kernel, in_specs=[spec], out_specs=[spec, spec],...  4.91 us
    ppermute x1, starting transfers between devices, per_device(): earlier = lax.ppermute(tail, 'img', [(i, i + 1) for i in range(count - 1)])  4.73 us
  transfers between devices with their start and end apart: 4, of which 3 were waited for; matrix products, arithmetic and copies ran while one was open for 0% of the time, Pallas kernels for 35%

profile of v5, /device:TPU:1, one launch (start us, length us, event | category | flops | bytes accessed | tf_op | source)
XLA Modules:
  0.0 122.0 jit_solution(10858832021931249164)
XLA Ops:
  0.6 1.2 %slice.3 = f32[2,32,3,384]{3,2,1,0:T(4,128)S(1)} slice(f32[2,32,32,384]{3,2,1,0:T(8,128)} %volt.1), slice={[0:2], [0:32], [29:32], [0:384]} | slice | bytes 589824 | tf_op jit(solution)/shard_map/slice | solution.py:652
  1.9 0.0 copy-start.7
  1.9 0.0 copy-start.2
  1.9 0.0 copy-start.3
  1.9 4.7 %collective-permute-start = (f32[2,3,32,384]{3,2,1,0:T(8,128)S(1)}, f32[2,3,32,384]{3,2,1,0:T(8,128)S(1)}, u32[]{:S(2)}, u32[]{:S(2)}) collective-permute-start(f32[2,3,32,384]{3,2,1,0:T(8,128)S(1)} %bitcast.28), channel_id=1, source_target_pairs={{0,1},{1,2},{2,3},{3,4},{4,5},{5,6},{6,7},{8,9},{9,10},{10,11},{11... | collective-permute-start | bytes 884744 | tf_op jit(solution)/shard_map/ppermute | solution.py:654
  6.7 3.6 %collective-permute-done.halo = f32[2,3,32,384]{3,2,1,0:T(8,128)S(1)} collective-permute-done((f32[2,3,32,384]{3,2,1,0:T(8,128)S(1)}, f32[2,3,32,384]{3,2,1,0:T(8,128)S(1)}, u32[]{:S(2)}, u32[]{:S(2)}) %collective-permute-start) | collective-permute-done | bytes 294944 | tf_op jit(solution)/shard_map/ppermute | solution.py:654
  10.3 0.7 copy-done.8
  11.0 6.7 %channelizer.1 = f32[2048,128]{1,0:T(8,128)} custom-call(f32[2,32,32,384]{3,2,1,0:T(8,128)} %volt.1, f32[2,3,32,384]{3,2,1,0:T(8,128)} %copy-done.8, f32[4,384]{1,0:T(4,128)} %proto.1, bf16[256,768]{1,0:T(8,128)(2,1)} %constant.6.clone.table_high, bf16[256,768]{1,0:T(8,128)(2,1)} %constant.7.clone.table_low), custom_call_target="tpu_custom_call" | custom-call | flops 1200000000 | bytes 6000000 | tf_op jit(solution)/shard_map/channelizer/pallas_call | solution.py:83
  17.7 11.3 %all-to-all-start = ((f32[128,1,2048]{2,1,0:T(1,128)}), f32[128,1,2048]{2,1,0:T(1,128)S(1)}, u32[]{:S(2)}, u32[]{:S(2)}) async-start(f32[128,1,2048]{2,1,0:T(1,128)} %bitcast.26), calls=%async_computation | async-start | bytes 2097152 | tf_op jit(solution)/shard_map/all_to_all | solution.py:645
  29.1 2.6 %record_starts.1.args_2_.args_3_ = s32[32,32]{1,0:T(8,128)} custom-call(s32[320,128]{1,0:T(8,128)} %bitcast.22), custom_call_target="tpu_custom_call" | custom-call | flops 100000000 | bytes 200000 | tf_op jit(solution)/shard_map/record_starts/pallas_call | solution.py:245
  31.7 0.7 copy-done.4
  32.4 13.0 %sort_places.1 = f32[1920,128]{1,0:T(8,128)} custom-call(f32[2,320,128]{2,1,0:T(8,128)S(1)} %bitcast.19, f32[1,320,128]{2,1,0:T(8,128)S(1)} %bitcast.25, s32[320,128]{1,0:T(8,128)S(1)} %bitcast.23, s32[32,32]{1,0:T(8,128)S(1)} %copy-done.4), custom_call_target="tpu_custom_call" | custom-call | flops 200000000 | bytes 9000000 | tf_op jit(solution)/shard_map/sort_places/pallas_call | solution.py:411
  45.4 2.7 %all-to-all-done = f32[128,1,2048]{2,1,0:T(1,128)S(1)} async-done(((f32[128,1,2048]{2,1,0:T(1,128)}), f32[128,1,2048]{2,1,0:T(1,128)S(1)}, u32[]{:S(2)}, u32[]{:S(2)}) %all-to-all-start) | async-done | bytes 1048608 | tf_op jit(solution)/shard_map/all_to_all | solution.py:645
  48.1 7.1 %all-to-all-start.2 = ((f32[128,1,1920]{2,1,0:T(1,128)}), f32[128,1,1920]{2,1,0:T(1,128)S(1)}, u32[]{:S(2)}, u32[]{:S(2)}) async-start(f32[128,1,1920]{2,1,0:T(1,128)} %bitcast.8), calls=%async_computation.2 | async-start | bytes 1966080 | tf_op jit(solution)/shard_map/all_to_all | solution.py:645
  55.2 4.9 %correlator.1 = (f32[10,2,128,128]{3,2,1,0:T(8,128)}, f32[2,320,128]{2,1,0:T(8,128)S(1)}) custom-call(f32[2048,128]{1,0:T(8,128)S(1)} %bitcast.20), custom_call_target="tpu_custom_call" | custom-call | flops 4000000000 | bytes 4000000 | tf_op jit(solution)/shard_map/correlator/pallas_call | solution.py:192
  60.1 11.6 %sort_values.1 = f32[1280,128]{1,0:T(8,128)} custom-call(f32[2,320,128]{2,1,0:T(8,128)S(1)} %get-tuple-element.7.args_0_, s32[320,128]{1,0:T(8,128)S(1)} %bitcast.24, s32[32,32]{1,0:T(8,128)S(1)} %copy-done.5), custom_call_target="tpu_custom_call" | custom-call | flops 200000000 | bytes 6000000 | tf_op jit(solution)/shard_map/sort_values/pallas_call | solution.py:411
  71.8 1.8 %all-to-all-done.2 = f32[128,1,1920]{2,1,0:T(1,128)S(1)} async-done(((f32[128,1,1920]{2,1,0:T(1,128)}), f32[128,1,1920]{2,1,0:T(1,128)S(1)}, u32[]{:S(2)}, u32[]{:S(2)}) %all-to-all-start.2) | async-done | bytes 983072 | tf_op jit(solution)/shard_map/all_to_all | solution.py:645
  73.6 8.0 %all-to-all-start.1 = ((f32[128,1,1280]{2,1,0:T(1,128)}), f32[128,1,1280]{2,1,0:T(1,128)S(1)}, u32[]{:S(2)}, u32[]{:S(2)}) async-start(f32[128,1,1280]{2,1,0:T(1,128)} %bitcast.5), calls=%async_computation.1 | async-start | bytes 1310720 | tf_op jit(solution)/shard_map/all_to_all | solution.py:645
  81.5 0.0 copy-start.6
  81.6 10.5 %right_tables.1 = (bf16[40,128,2048]{2,1,0:T(8,128)(2,1)S(1)}, f32[3,640,128]{2,1,0:T(8,128)S(1)}) custom-call(f32[1920,128]{1,0:T(8,128)S(1)} %bitcast.21), custom_call_target="tpu_custom_call" | custom-call | flops 3000000000 | bytes 22000000 | tf_op jit(solution)/shard_map/right_tables/pallas_call | solution.py:592
  92.1 7.0 %copy-done = bf16[40,128,2048]{2,1,0:T(8,128)(2,1)} copy-done((bf16[40,128,2048]{2,1,0:T(8,128)(2,1)}, bf16[40,128,2048]{2,1,0:T(8,128)(2,1)S(1)}, u32[]{:S(2)}) %copy-start) | copy-done | bytes 20971544
  99.1 7.0 %copy-done.1 = bf16[40,128,2048]{2,1,0:T(8,128)(2,1)S(1)} copy-done((bf16[40,128,2048]{2,1,0:T(8,128)(2,1)S(1)}, bf16[40,128,2048]{2,1,0:T(8,128)(2,1)}, u32[]{:S(2)}) %copy-start.1) | copy-done | bytes 20971544
  106.0 15.2 %gridding.1 = f32[8,2,32,32]{3,2,1,0:T(8,128)S(1)} custom-call(f32[1280,128]{1,0:T(8,128)S(1)} %bitcast.18, bf16[40,128,2048]{2,1,0:T(8,128)(2,1)S(1)} %copy-done.1, f32[3,640,128]{2,1,0:T(8,128)S(1)} %get-tuple-element.9.table, f32[64,64]{1,0:T(8,128)S(1)} %copy-done.6), custom_call_target="tpu_custom_call" | custom-call | flops 3000000000 | bytes 25000000 | tf_op jit(solution)/shard_map/gridding/pallas_call | solution.py:618
  121.2 0.8 reshape.43
  (13 shorter events, 0.1 us)
Async XLA Ops:
  1.9 27.1 %copy-start.7 = (f32[2,40960]{1,0:T(2,128)S(1)}, f32[2,40960]{1,0:T(2,128)}, u32[]{:S(2)}) copy-start(f32[2,40960]{1,0:T(2,128)} %param.10) | copy-start | bytes 983044
  1.9 29.8 %copy-start.2 = (s32[40960,1]{0,1:T(1,128)S(1)}, s32[40960,1]{0,1:T(1,128)}, u32[]{:S(2)}) copy-start(s32[40960,1]{0,1:T(1,128)} %param.12) | copy-start | bytes 491524
  1.9 29.8 %copy-start.3 = (f32[40960]{0:T(1024)S(1)}, f32[40960]{0:T(1024)}, u32[]{:S(2)}) copy-start(f32[40960]{0:T(1024)} %param.11) | copy-start | bytes 491524
  1.9 8.4 %collective-permute-start = (f32[2,3,32,384]{3,2,1,0:T(8,128)S(1)}, f32[2,3,32,384]{3,2,1,0:T(8,128)S(1)}, u32[]{:S(2)}, u32[]{:S(2)}) collective-permute-start(f32[2,3,32,384]{3,2,1,0:T(8,128)S(1)} %bitcast.28), channel_id=1, source_target_pairs={{0,1},{1,2},{2,3},{3,4},{4,5},{5,6},{6,7},{8,9},{9,10},{10,11},{11... | collective-permute-start | bytes 884744 | tf_op jit(solution)/shard_map/ppermute | solution.py:654
  10.3 0.7 copy-start.8
  17.7 30.4 %all-to-all-start = ((f32[128,1,2048]{2,1,0:T(1,128)}), f32[128,1,2048]{2,1,0:T(1,128)S(1)}, u32[]{:S(2)}, u32[]{:S(2)}) async-start(f32[128,1,2048]{2,1,0:T(1,128)} %bitcast.26), calls=%async_computation | async-start | bytes 2097152 | tf_op jit(solution)/shard_map/all_to_all | solution.py:645
  31.7 0.7 copy-start.4
  48.1 25.5 %all-to-all-start.2 = ((f32[128,1,1920]{2,1,0:T(1,128)}), f32[128,1,1920]{2,1,0:T(1,128)S(1)}, u32[]{:S(2)}, u32[]{:S(2)}) async-start(f32[128,1,1920]{2,1,0:T(1,128)} %bitcast.8), calls=%async_computation.2 | async-start | bytes 1966080 | tf_op jit(solution)/shard_map/all_to_all | solution.py:645
  55.2 4.9 %copy-start.5 = (s32[32,32]{1,0:T(8,128)S(1)}, s32[32,32]{1,0:T(8,128)}, u32[]{:S(2)}) copy-start(s32[32,32]{1,0:T(8,128)} %record_starts.1.args_2_.args_3_) | copy-start | bytes 12292
  73.6 25.5 %all-to-all-start.1 = ((f32[128,1,1280]{2,1,0:T(1,128)}), f32[128,1,1280]{2,1,0:T(1,128)S(1)}, u32[]{:S(2)}, u32[]{:S(2)}) async-start(f32[128,1,1280]{2,1,0:T(1,128)} %bitcast.5), calls=%async_computation.1 | async-start | bytes 1310720 | tf_op jit(solution)/shard_map/all_to_all | solution.py:645
  81.5 17.5 %copy-start.6 = (f32[64,64]{1,0:T(8,128)S(1)}, f32[64,64]{1,0:T(8,128)}, u32[]{:S(2)}) copy-start(f32[64,64]{1,0:T(8,128)} %constant.8.clone.mix) | copy-start | bytes 49156
  92.1 7.0 %copy-start = (bf16[40,128,2048]{2,1,0:T(8,128)(2,1)}, bf16[40,128,2048]{2,1,0:T(8,128)(2,1)S(1)}, u32[]{:S(2)}) copy-start(bf16[40,128,2048]{2,1,0:T(8,128)(2,1)S(1)} %get-tuple-element.8.right) | copy-start | bytes 62914564
  99.1 7.0 %copy-start.1 = (bf16[40,128,2048]{2,1,0:T(8,128)(2,1)S(1)}, bf16[40,128,2048]{2,1,0:T(8,128)(2,1)}, u32[]{:S(2)}) copy-start(bf16[40,128,2048]{2,1,0:T(8,128)(2,1)} %copy-done) | copy-start | bytes 62914564
